TPU v7x, 512 devices: a whole 4x8x8 slice. The times are simulated.
512 devices in a mesh: section: 8 (over x, y_hi), dp: 64 (over z, y_lo, core).
Axes of the slice: x: 4, y: 8 (y_hi: 2, y_lo: 4; y = y_hi * 4 + y_lo), z: 8, core: 2. Of those that a mesh axis runs over, the one named last changes fastest.
Arguments:
- stream_in: bfloat16 [8, 49344, 768], P('section', 'dp'), may hold values from -20 to 20
- timestep: int32 [192], P('dp'), may hold values from 0 to 999
- ln_gain: float32 [8, 768], P('section'), may hold values from 0.25 to 1.75
- qkv_weight: bfloat16 [8, 768, 2304], P('section', 'dp'), may hold values from -4 to 4
- out_weight: bfloat16 [8, 768, 768], P('section', 'dp'), may hold values from -0.75 to 0.75
- join_weight: bfloat16 [4, 1536, 768], P(None, 'dp'), may hold values from -0.15625 to 0.15625
- ctx_saved: bfloat16 [8, 49344, 768], P('section', 'dp'), may hold values from -16 to 16
- out_cot: bfloat16 [8, 49344, 768], P('section', 'dp'), may hold values from -0.02734375 to 0.02734375
Outputs:
- stream_out: bfloat16 [8, 49344, 768], P('section', 'dp')
- weight_grad: float32 [8, 768, 768], P('section', 'dp')
All inputs are finite; a program needn't handle non-finite values.
Results may differ from a plain program's by a relative error of at most 0.013.
Values may be sent and summed in bfloat16 or wider, within the bound.
No kernel may reach another device: no remote copies, remote signals or barrier semaphores. Data moves between devices by JAX's collectives and lax.ppermute only.
A program may use at most 128 MiB of HBM per device.

v0:
```python
import math

import jax
import jax.numpy as jnp
from jax import lax
from jax.sharding import PartitionSpec as P

D = 768
HEADS = 12
HEAD_DIM = 64
SEQ = 257


def from_behind(block, axis, distance):
    devices = range(lax.axis_size(axis))
    route = [((i - distance) % len(devices), i) for i in devices]
    return lax.ppermute(block, axis, route)


def time_rows(timestep):
    half_width = D // 2
    frequency = jnp.exp(
        -math.log(10000.0) * jnp.arange(half_width).astype(jnp.float32) / half_width
    )
    angles = timestep.astype(jnp.float32)[:, None] * frequency[None, :]
    return jnp.concatenate([jnp.cos(angles), jnp.sin(angles)], axis=1).astype(jnp.bfloat16)


def normalize(values, gain_row):
    floats = values.astype(jnp.float32)
    center = jnp.mean(floats, axis=-1, keepdims=True)
    spread = jnp.mean(jnp.square(floats - center), axis=-1, keepdims=True)
    return ((floats - center) * lax.rsqrt(spread + 1e-05) * gain_row).astype(jnp.bfloat16)


def attend(qkv_rows, head_count, batch_count):
    shaped = qkv_rows.reshape(batch_count, SEQ, 3, head_count, HEAD_DIM)
    queries = shaped[:, :, 0]
    key_rows = shaped[:, :, 1]
    value_rows = shaped[:, :, 2]
    scores = jnp.einsum(
        "bqhd,bkhd->bhqk", queries, key_rows, preferred_element_type=jnp.float32
    ) * HEAD_DIM ** (-0.5)
    row_max = jnp.max(scores, axis=-1, keepdims=True)
    powered = jnp.exp(scores - row_max)
    weights_soft = (powered / jnp.sum(powered, axis=-1, keepdims=True)).astype(jnp.bfloat16)
    context = jnp.einsum(
        "bhqk,bkhd->bqhd", weights_soft, value_rows, preferred_element_type=jnp.float32
    )
    return context.astype(jnp.bfloat16).reshape(batch_count * SEQ, head_count * HEAD_DIM)


def on_device(
    stream_in, timestep, ln_gain, qkv_weight, out_weight, join_weight, ctx_saved, out_cot
):
    section_count = lax.axis_size("section")
    half_count = section_count // 2
    section_index = lax.axis_index("section")
    entering = stream_in[0]
    row_count = entering.shape[0]
    image_count = row_count // SEQ
    sliced = entering.reshape(row_count, section_count, D // section_count)
    spread_out = lax.all_to_all(sliced, "section", split_axis=1, concat_axis=1, tiled=True)
    reordered = jnp.roll(jnp.flip(spread_out, 1), 1, axis=1)
    mirrored = lax.all_to_all(
        reordered, "section", split_axis=1, concat_axis=1, tiled=True
    ).reshape(row_count, D)
    by_image = entering.reshape(image_count, SEQ, D)
    first_rows = jnp.where(section_index == 0, time_rows(timestep), by_image[:, 0, :])
    entering = by_image.at[:, 0, :].set(first_rows).reshape(row_count, D)
    join_local = lax.dynamic_index_in_dim(
        join_weight, jnp.maximum(section_index - half_count, 0), 0, keepdims=False
    )
    qkv_matrix, out_matrix, join_matrix = (
        lax.all_gather(qkv_weight[0], "dp", axis=0, tiled=True),
        lax.all_gather(out_weight[0], "dp", axis=0, tiled=True),
        lax.all_gather(join_local, "dp", axis=0, tiled=True),
    )

    def join_inputs():
        mixed_sum = jnp.dot(entering, join_matrix[:D], preferred_element_type=jnp.float32)
        mixed_sum = mixed_sum + jnp.dot(
            mirrored, join_matrix[D:], preferred_element_type=jnp.float32
        )
        return mixed_sum.astype(jnp.bfloat16)

    def keep_inputs():
        return entering

    block_in = lax.cond(section_index >= half_count, join_inputs, keep_inputs)
    normed = normalize(block_in, ln_gain[0])
    qkv_rows = jnp.dot(normed, qkv_matrix, preferred_element_type=jnp.float32).astype(jnp.bfloat16)
    context = attend(qkv_rows, HEADS, image_count)
    projected = jnp.dot(context, out_matrix, preferred_element_type=jnp.float32)
    block_out = (block_in.astype(jnp.float32) + projected).astype(jnp.bfloat16)
    stream_out = from_behind(block_out, "section", 1)
    saved_rows = ctx_saved[0]
    cot_rows = out_cot[0]
    weight_grad = lax.psum_scatter(
        lax.dot_general(
            saved_rows, cot_rows, (((0,), (0,)), ((), ())), preferred_element_type=jnp.float32
        ),
        "dp",
        scatter_dimension=0,
        tiled=True,
    )
    return (stream_out[None], weight_grad[None])


def solution(mesh):
    return jax.shard_map(
        on_device,
        mesh=mesh,
        in_specs=(
            P("section", "dp", None),
            P("dp"),
            P("section", None),
            P("section", "dp", None),
            P("section", "dp", None),
            P(None, "dp", None),
            P("section", "dp", None),
            P("section", "dp", None),
        ),
        out_specs=(P("section", "dp", None), P("section", "dp", None)),
        check_vma=False,
    )
```

profile of v0, /device:TPU:1, one launch (start us, length us, event | category | flops | bytes accessed | tf_op | source)
XLA Modules:
  0.0 698.8 jit_solution(14378196088724731324)
XLA Ops:
  12.9 41.0 %all_to_all.10 = bf16[771,8,96]{0,2,1:T(8,128)(2,1)S(1)} all-to-all(bf16[771,8,96]{0,2,1:T(8,128)(2,1)} %bitcast.43), channel_id=1, replica_groups=mesh['section'=8,'dp'=64] {'section'}, dimensions={1} | all-to-all | bytes 2368512 | tf_op jit(solution)/shard_map/all_to_all | solution.py:63
  57.5 2.5 pad_maximum_fusion
  60.0 4.4 all-to-all-start.1
  68.4 4.2 fusion.19
  72.6 10.4 %all-to-all-done.1 = bf16[771,8,96]{0,2,1:T(8,128)(2,1)} async-done(((bf16[771,8,96]{0,2,1:T(8,128)(2,1)}), bf16[771,8,96]{0,2,1:T(8,128)(2,1)}, u32[]{:S(2)}, u32[]{:S(2)}) %all-to-all-start.1) | async-done | bytes 1184288 | tf_op jit(solution)/shard_map/all_to_all | solution.py:65
  83.0 93.1 %all-gather.7.cloned.1.call-done = bf16[1,1536,768]{2,1,0:T(8,128)(2,1)} async-done(((bf16[1,24,768]{2,1,0:T(8,128)(2,1)}), bf16[1,1536,768]{2,1,0:T(8,128)(2,1)}) %all-gather.7.cloned.1.call-update) | async-done | bytes 2359312 | tf_op jit(solution)/shard_map/all_gather | solution.py:77
  178.3 120.8 %all-gather.9.cloned.1.call-done = bf16[1,768,2304]{2,0,1:T(2,128)(2,1)} async-done(((bf16[1,12,2304]{2,0,1:T(2,128)(2,1)}), bf16[1,768,2304]{2,0,1:T(2,128)(2,1)}) %all-gather.9.cloned.1.call-update) | async-done | bytes 3538960 | tf_op jit(solution)/shard_map/all_gather | solution.py:75
  299.1 8.7 %convolution_convert_fusion = bf16[771,2304]{1,0:T(8,128)(2,1)} fusion(bf16[1,768,2304]{2,0,1:T(2,128)(2,1)} %all-gather.9.cloned.1.call-done, f32[771,768]{1,0:T(8,128)} %copy-done.2, f32[768]{0:T(1024)S(1)} %reduce.2, f32[771]{0:T(1024)S(1)} %add_rsqrt_fusion, f32[771]{0:T(1024)S(1)} %broadcast_multiply_fusion), kind=kOutput, calls=%fused_computation.12 | convolution fusion | flops 2732670720 | bytes 9469464 | tf_op jit(solution)/shard_map/dot_general | solution.py:92
  307.8 11.8 %reshape.139 = bf16[3,257,3,12,64]{4,3,2,1,0:T(8,128)(2,1)} reshape(bf16[771,2304]{1,0:T(8,128)(2,1)} %convolution_convert_fusion) | data formatting | bytes 7105536 | tf_op jit(solution)/shard_map/reshape | solution.py:37
  319.6 7.1 %fusion.34 = (bf16[3,257,1,12,64]{4,3,2,1,0:T(8,128)(2,1)}, bf16[3,257,1,12,64]{4,3,2,1,0:T(8,128)(2,1)}, bf16[3,257,1,12,64]{4,3,2,1,0:T(8,128)(2,1)}) fusion(bf16[3,257,3,12,64]{4,3,2,1,0:T(8,128)(2,1)} %reshape.139), kind=kLoop, calls=%fused_computation.47 | loop fusion | bytes 7105536 | tf_op jit(solution)/shard_map/slice | solution.py:40
  326.7 5.6 copy.73
  332.3 5.7 copy.74
  338.0 9.4 %fusion.13 = f32[3,12,257,257]{2,3,1,0:T(8,128)} fusion(bf16[3,257,1,12,64]{1,4,3,0,2:T(8,128)(2,1)} %copy.74, bf16[3,257,1,12,64]{1,4,3,0,2:T(8,128)(2,1)S(1)} %copy.73), kind=kOutput, calls=%fused_computation.18 | convolution fusion | flops 304353792 | bytes 11879568 | tf_op jit(solution)/shard_map/bqhd,bkhd->bhqk/dot_general | solution.py:41
  347.5 18.4 %fusion.35 = (f32[3,12,257]{2,1,0:T(8,128)S(1)}, f32[3,12,257,257]{2,3,1,0:T(8,128)}) fusion(f32[3,12,257,257]{2,3,1,0:T(8,128)} %fusion.13), kind=kOutput, calls=%fused_computation.48 | output fusion | flops 9511312 | bytes 19059120 | tf_op jit(solution)/shard_map/sub | solution.py:45
  365.9 5.6 copy.72
  371.5 7.1 %convert_bitcast_fusion = bf16[3,257,12,64]{1,3,2,0:T(8,128)(2,1)S(1)} fusion(f32[3,12,257,257]{2,3,1,0:T(8,128)} %get-tuple-element.75, f32[3,12,257]{2,1,0:T(8,128)S(1)} %get-tuple-element.74, bf16[3,257,1,12,64]{1,4,3,0,2:T(8,128)(2,1)S(1)} %copy.72), kind=kOutput, calls=%fused_computation.22 | convolution fusion | flops 309701440 | bytes 11916576 | tf_op jit(solution)/shard_map/bhqk,bkhd->bqhd/dot_general | solution.py:47
  380.1 2.7 reshape.133
  382.8 35.7 %all-gather.11.cloned.1.call-done = bf16[1,768,768]{2,0,1:T(2,128)(2,1)} async-done(((bf16[1,12,768]{2,0,1:T(2,128)(2,1)}), bf16[1,768,768]{2,0,1:T(2,128)(2,1)}) %all-gather.11.cloned.1.call-update) | async-done | bytes 1179664 | tf_op jit(solution)/shard_map/all_gather | solution.py:76
  418.5 5.0 add_convert_fusion.1
  423.4 7.1 %collective-permute-start = (bf16[771,768]{1,0:T(8,128)(2,1)}, bf16[771,768]{1,0:T(8,128)(2,1)}, u32[]{:S(2)}, u32[]{:S(2)}) collective-permute-start(bf16[771,768]{1,0:T(8,128)(2,1)} %add_convert_fusion.1), channel_id=1, source_target_pairs={{448,0},{0,64},{64,128},{128,192},{192,256},{256,320},{320,384},{3... | collective-permute-start | bytes 3552776 | tf_op jit(solution)/shard_map/ppermute | solution.py:17
  430.5 194.8 %fusion = f32[16,768]{1,0:T(8,128)} fusion(f32[768,768]{1,0:T(8,128)S(1)} %copy-done.4), kind=kCustom, calls=%all-reduce-scatter | all-reduce-scatter fusion | flops 786433 | bytes 2410496
  625.4 3.5 collective-permute-start.1
  632.2 2.8 collective-permute-start.16
  636.2 7.4 %collective-permute-start.12 = (f32[16,768]{1,0:T(8,128)}, f32[16,768]{1,0:T(8,128)S(1)}, u32[]{:S(2)}, u32[]{:S(2)}) collective-permute-start(f32[16,768]{1,0:T(8,128)} %fusion), channel_id=1, source_target_pairs={{0,12},{1,13},{2,14},{3,15},{4,16},{5,17},{6,18},{7,19},{8,20},{9,... | collective-permute-start | bytes 147464
  643.7 13.8 %collective-permute-start.13 = (f32[16,768]{1,0:T(8,128)}, f32[16,768]{1,0:T(8,128)S(1)}, u32[]{:S(2)}, u32[]{:S(2)}) collective-permute-start(f32[16,768]{1,0:T(8,128)} %fusion), channel_id=1, source_target_pairs={{0,13},{1,14},{2,15},{3,16},{4,17},{5,18},{6,19},{7,20},{8,21},{9,... | collective-permute-start | bytes 147464
  662.2 4.2 collective-permute-start.3
  666.5 4.0 collective-permute-start.4
  670.5 2.8 collective-permute-start.5
  674.9 4.3 collective-permute-start.7
  679.2 2.7 collective-permute-start.8
  681.9 2.5 collective-permute-start.9
  686.4 2.8 concatenate.23
  (73 shorter events, 32.3 us)
Async XLA Ops:
  7.2 61.2 %copy-start = (bf16[1,771,768]{2,1,0:T(8,128)(2,1)S(1)}, bf16[1,771,768]{2,1,0:T(8,128)(2,1)}, u32[]{:S(2)}) copy-start(bf16[1,771,768]{2,1,0:T(8,128)(2,1)} %param.19) | copy-start | bytes 3552772
  7.2 168.9 %all-gather.7.cloned.1.call-start = ((), (), s32[]{:S(2)}) async-start(), calls=%async_computation.2 | async-start | bytes 2396160 | tf_op jit(solution)/shard_map/all_gather | solution.py:77
  8.7 290.4 %all-gather.9.cloned.1.call-start = ((), (), s32[]{:S(2)}) async-start(), calls=%async_computation.3 | async-start | bytes 7188480 | tf_op jit(solution)/shard_map/all_gather | solution.py:75
  57.5 7.0 %copy-start.5 = (bf16[1,12,768]{2,1,0:T(8,128)(2,1)S(1)}, bf16[1,12,768]{2,1,0:T(8,128)(2,1)}, u32[]{:S(2)}) copy-start(bf16[1,12,768]{2,1,0:T(8,128)(2,1)} %param.16) | copy-start | bytes 55300
  60.0 6.7 copy-start.8
  60.0 23.0 %all-to-all-start.1 = ((bf16[771,8,96]{0,2,1:T(8,128)(2,1)}), bf16[771,8,96]{0,2,1:T(8,128)(2,1)}, u32[]{:S(2)}, u32[]{:S(2)}) async-start(bf16[771,8,96]{0,2,1:T(8,128)(2,1)} %pad_maximum_fusion), calls=%async_computation.1 | async-start | bytes 2752512 | tf_op jit(solution)/shard_map/all_to_all | solution.py:65
  64.4 354.1 %all-gather.11.cloned.1.call-start = ((), (), s32[]{:S(2)}) async-start(), calls=%async_computation.4 | async-start | bytes 2396160 | tf_op jit(solution)/shard_map/all_gather | solution.py:76
  65.2 3.2 copy-start.6
  68.4 107.7 %copy-start.3 = (bf16[771,768]{1,0:T(8,128)(2,1)S(1)}, bf16[771,768]{1,0:T(8,128)(2,1)}, u32[]{:S(2)}) copy-start(bf16[771,768]{1,0:T(8,128)(2,1)} %reshape.131) | copy-start | bytes 3552772
  176.5 1.4 copy-start.2
  382.8 47.7 %copy-start.4 = (f32[768,768]{1,0:T(8,128)S(1)}, f32[768,768]{1,0:T(8,128)}, u32[]{:S(2)}) copy-start(f32[768,768]{1,0:T(8,128)} %fusion.19) | copy-start | bytes 7077892
  423.4 266.4 %collective-permute-start = (bf16[771,768]{1,0:T(8,128)(2,1)}, bf16[771,768]{1,0:T(8,128)(2,1)}, u32[]{:S(2)}, u32[]{:S(2)}) collective-permute-start(bf16[771,768]{1,0:T(8,128)(2,1)} %add_convert_fusion.1), channel_id=1, source_target_pairs={{448,0},{0,64},{64,128},{128,192},{192,256},{256,320},{320,384},{3... | collective-permute-start | bytes 3552776 | tf_op jit(solution)/shard_map/ppermute | solution.py:17
  430.5 261.7 %copy-start.1 = (bf16[1,771,768]{2,1,0:T(8,128)(2,1)S(1)}, bf16[1,771,768]{2,1,0:T(8,128)(2,1)}, u32[]{:S(2)}) copy-start(bf16[1,771,768]{2,1,0:T(8,128)(2,1)} %param.19) | copy-start | bytes 3552772
  625.4 18.3 %collective-permute-start.1 = (f32[16,768]{1,0:T(8,128)}, f32[16,768]{1,0:T(8,128)S(1)}, u32[]{:S(2)}, u32[]{:S(2)}) collective-permute-start(f32[16,768]{1,0:T(8,128)} %fusion), channel_id=1, source_target_pairs={{0,1},{1,2},{2,3},{3,4},{4,5},{5,6},{6,7},{7,8},{8,9},{9,10},{10,1... | collective-permute-start | bytes 147464
  628.8 28.7 %collective-permute-start.10 = (f32[16,768]{1,0:T(8,128)}, f32[16,768]{1,0:T(8,128)S(1)}, u32[]{:S(2)}, u32[]{:S(2)}) collective-permute-start(f32[16,768]{1,0:T(8,128)} %fusion), channel_id=1, source_target_pairs={{0,10},{1,11},{2,12},{3,13},{4,14},{5,15},{6,16},{7,17},{8,18},{9,... | collective-permute-start | bytes 147464
  630.1 28.7 %collective-permute-start.11 = (f32[16,768]{1,0:T(8,128)}, f32[16,768]{1,0:T(8,128)S(1)}, u32[]{:S(2)}, u32[]{:S(2)}) collective-permute-start(f32[16,768]{1,0:T(8,128)} %fusion), channel_id=1, source_target_pairs={{0,11},{1,12},{2,13},{3,14},{4,15},{5,16},{6,17},{7,18},{8,19},{9,... | collective-permute-start | bytes 147464
  632.2 4.0 collective-permute-start.16
  636.2 23.9 %collective-permute-start.12 = (f32[16,768]{1,0:T(8,128)}, f32[16,768]{1,0:T(8,128)S(1)}, u32[]{:S(2)}, u32[]{:S(2)}) collective-permute-start(f32[16,768]{1,0:T(8,128)} %fusion), channel_id=1, source_target_pairs={{0,12},{1,13},{2,14},{3,15},{4,16},{5,17},{6,18},{7,19},{8,20},{9,... | collective-permute-start | bytes 147464
  643.7 18.6 %collective-permute-start.13 = (f32[16,768]{1,0:T(8,128)}, f32[16,768]{1,0:T(8,128)S(1)}, u32[]{:S(2)}, u32[]{:S(2)}) collective-permute-start(f32[16,768]{1,0:T(8,128)} %fusion), channel_id=1, source_target_pairs={{0,13},{1,14},{2,15},{3,16},{4,17},{5,18},{6,19},{7,20},{8,21},{9,... | collective-permute-start | bytes 147464
  657.5 9.0 %collective-permute-start.14 = (f32[16,768]{1,0:T(8,128)}, f32[16,768]{1,0:T(8,128)S(1)}, u32[]{:S(2)}, u32[]{:S(2)}) collective-permute-start(f32[16,768]{1,0:T(8,128)} %fusion), channel_id=1, source_target_pairs={{0,14},{1,15},{2,16},{3,17},{4,18},{5,19},{6,20},{7,21},{8,22},{9,... | collective-permute-start | bytes 147464
  658.8 11.7 %collective-permute-start.15 = (f32[16,768]{1,0:T(8,128)}, f32[16,768]{1,0:T(8,128)S(1)}, u32[]{:S(2)}, u32[]{:S(2)}) collective-permute-start(f32[16,768]{1,0:T(8,128)} %fusion), channel_id=1, source_target_pairs={{0,15},{1,16},{2,17},{3,18},{4,19},{5,20},{6,21},{7,22},{8,23},{9,... | collective-permute-start | bytes 147464
  660.1 13.2 %collective-permute-start.2 = (f32[16,768]{1,0:T(8,128)}, f32[16,768]{1,0:T(8,128)S(1)}, u32[]{:S(2)}, u32[]{:S(2)}) collective-permute-start(f32[16,768]{1,0:T(8,128)} %fusion), channel_id=1, source_target_pairs={{0,2},{1,3},{2,4},{3,5},{4,6},{5,7},{6,8},{7,9},{8,10},{9,11},{10,... | collective-permute-start | bytes 147464
  662.2 12.7 %collective-permute-start.3 = (f32[16,768]{1,0:T(8,128)}, f32[16,768]{1,0:T(8,128)S(1)}, u32[]{:S(2)}, u32[]{:S(2)}) collective-permute-start(f32[16,768]{1,0:T(8,128)} %fusion), channel_id=1, source_target_pairs={{0,3},{1,4},{2,5},{3,6},{4,7},{5,8},{6,9},{7,10},{8,11},{9,12},{10... | collective-permute-start | bytes 147464
  666.5 12.7 %collective-permute-start.4 = (f32[16,768]{1,0:T(8,128)}, f32[16,768]{1,0:T(8,128)S(1)}, u32[]{:S(2)}, u32[]{:S(2)}) collective-permute-start(f32[16,768]{1,0:T(8,128)} %fusion), channel_id=1, source_target_pairs={{0,4},{1,5},{2,6},{3,7},{4,8},{5,9},{6,10},{7,11},{8,12},{9,13},{1... | collective-permute-start | bytes 147464
  670.5 11.4 %collective-permute-start.5 = (f32[16,768]{1,0:T(8,128)}, f32[16,768]{1,0:T(8,128)S(1)}, u32[]{:S(2)}, u32[]{:S(2)}) collective-permute-start(f32[16,768]{1,0:T(8,128)} %fusion), channel_id=1, source_target_pairs={{0,5},{1,6},{2,7},{3,8},{4,9},{5,10},{6,11},{7,12},{8,13},{9,14},{... | collective-permute-start | bytes 147464
  673.3 13.0 %collective-permute-start.6 = (f32[16,768]{1,0:T(8,128)}, f32[16,768]{1,0:T(8,128)S(1)}, u32[]{:S(2)}, u32[]{:S(2)}) collective-permute-start(f32[16,768]{1,0:T(8,128)} %fusion), channel_id=1, source_target_pairs={{0,6},{1,7},{2,8},{3,9},{4,10},{5,11},{6,12},{7,13},{8,14},{9,15},... | collective-permute-start | bytes 147464
  674.9 11.4 %collective-permute-start.7 = (f32[16,768]{1,0:T(8,128)}, f32[16,768]{1,0:T(8,128)S(1)}, u32[]{:S(2)}, u32[]{:S(2)}) collective-permute-start(f32[16,768]{1,0:T(8,128)} %fusion), channel_id=1, source_target_pairs={{0,7},{1,8},{2,9},{3,10},{4,11},{5,12},{6,13},{7,14},{8,15},{9,16}... | collective-permute-start | bytes 147464
  679.2 7.2 %collective-permute-start.8 = (f32[16,768]{1,0:T(8,128)}, f32[16,768]{1,0:T(8,128)S(1)}, u32[]{:S(2)}, u32[]{:S(2)}) collective-permute-start(f32[16,768]{1,0:T(8,128)} %fusion), channel_id=1, source_target_pairs={{0,8},{1,9},{2,10},{3,11},{4,12},{5,13},{6,14},{7,15},{8,16},{9,17... | collective-permute-start | bytes 147464
  681.9 4.5 collective-permute-start.9
Sparse Core Ops, SparseCore 0:
  10.7 165.3 all-gather.6
  178.3 120.8 all-gather.8
  301.3 117.1 all-gather.10
where the time goes:
time: 700 us; the launch traced here: 699 us
  waiting for transfers between devices  261 us (37%)
  blocking collectives  236 us (34%)
  starting transfers between devices  68.4 us (10%)
  local copies, waits for them, and re-layouts  62.2 us (9%)
  matrix products  34.4 us (5%)
  other arithmetic  21.9 us (3%)
  between operations  14.9 us (2%)
    unnamed x1, blocking collectives  195 us
    all_gather x1, waiting for transfers between devices, on_device(): lax.all_gather(qkv_weight[0], 'dp', axis=0, tiled=True)  121 us
    all_gather x1, waiting for transfers between devices, on_device(): lax.all_gather(join_local, 'dp', axis=0, tiled=True)  93.1 us
    unnamed x16, starting transfers between devices  56.8 us
    all_to_all x1, blocking collectives, on_device(): lax.all_to_all(sliced, 'section', split_axis=1, concat_axis=1, tiled=True)  41 us
    all_gather x1, waiting for transfers between devices, on_device(): lax.all_gather(out_weight[0], 'dp', axis=0, tiled=True)  35.7 us
    unnamed x27, local copies, waits for them, and re-layouts  31 us
    sub x1, other arithmetic, attend(): powered = jnp.exp(scores - row_max)  18.4 us
  transfers between devices with their start and end apart: 21, of which 5 were waited for; matrix products, arithmetic and copies ran while one was open for 43% of the time, Pallas kernels for 0%

commit v1 on v0

v1 whole, which is shorter than its diff:
```python
import math

import jax
import jax.numpy as jnp
from jax import lax
from jax.experimental import pallas as pl
from jax.experimental.pallas import tpu as pltpu
from jax.sharding import Mesh
from jax.sharding import PartitionSpec as P

D = 768
HEADS = 12
HEAD_DIM = 64
SEQ = 257
PAD = 272
KEYS = 384
CUT = 112
SECTIONS = 8
REPLICAS = 64
AXES = ("x", "yh", "z", "yl", "c")
SECTION = ("x", "yh")


def time_rows(timestep):
    half_width = D // 2
    frequency = jnp.exp(
        -math.log(10000.0) * jnp.arange(half_width).astype(jnp.float32) / half_width
    )
    angles = timestep.astype(jnp.float32)[:, None] * frequency[None, :]
    return jnp.concatenate([jnp.cos(angles), jnp.sin(angles)], axis=1).astype(jnp.bfloat16)


def load_weights(place_ref, mine, other, w_qkv, w_out, w_join, sem):
    def copies(qkv_src, rest_src):
        made = []
        for z in range(8):
            rows = pl.ds(96 * z, 96)
            for part in range(3):
                made.append((qkv_src.at[z, pl.ds(96 * part, 96)], w_qkv.at[rows, pl.ds(D * part, D)]))
            made.append((rest_src.at[z, pl.ds(0, 96)], w_out.at[rows]))
            made.append((rest_src.at[z, pl.ds(96, 192)], w_join.at[pl.ds(192 * z, 192)]))
        return [pltpu.make_async_copy(s, d, sem.at[i]) for i, (s, d) in enumerate(made)]

    @pl.when(place_ref[0] == 0)
    def _():
        for copy in copies(mine, other):
            copy.start()

    @pl.when(place_ref[0] != 0)
    def _():
        for copy in copies(other, mine):
            copy.start()

    return copies(mine, other)


def block_kernel(
    images,
    first_image,
    pieces,
    place_ref,
    time_ref,
    gain_ref,
    mine,
    other,
    *refs,
):
    streams, skips, sides = (refs[i * len(pieces) : (i + 1) * len(pieces)] for i in range(3))
    out_ref, w_qkv, w_out, w_join, entering_rows, skip_rows, block_in, qkv_rows, context, sem = refs[
        3 * len(pieces) :
    ]
    section = place_ref[1]
    decoder = (section == 0) | (section >= 5)
    waits = load_weights(place_ref, mine, other, w_qkv, w_out, w_join, sem)
    qkv_rows[...] = jnp.zeros_like(qkv_rows)
    context[...] = jnp.zeros_like(context)
    for (image, start, count), stream, skip, side in zip(
        pieces, streams, skips, sides, strict=True
    ):
        rows = stream[...]
        if start == 0:
            first = lax.broadcasted_iota(jnp.int32, (count, D), 0) == 0
            token = time_ref[first_image + image].astype(jnp.bfloat16)
            rows = jnp.where(first & (section == 1), token, rows)
        entering_rows[image, start : start + count] = rows
        mirrored = jnp.where(section == 6, side[...], skip[...])
        skip_rows[image, start : start + count] = jnp.where(section == 5, rows, mirrored)
    for copy in waits:
        copy.wait()

    def one_image(image):
        entering = entering_rows[image]

        @pl.when(decoder)
        def _():
            mixed = jnp.dot(entering, w_join[:D], preferred_element_type=jnp.float32)
            mixed = mixed + jnp.dot(
                skip_rows[image], w_join[D:], preferred_element_type=jnp.float32
            )
            block_in[...] = mixed.astype(jnp.bfloat16)

        @pl.when(jnp.logical_not(decoder))
        def _():
            block_in[...] = entering

        floats = block_in[...].astype(jnp.float32)
        center = jnp.mean(floats, axis=-1, keepdims=True)
        moved = floats - center
        spread = jnp.mean(jnp.square(moved), axis=-1, keepdims=True)
        normed = (moved * lax.rsqrt(spread + 1e-05) * gain_ref[...]).astype(jnp.bfloat16)
        for part in range(3):
            columns = slice(D * part, D * part + D)
            qkv_rows[:SEQ, columns] = jnp.dot(
                normed, w_qkv[:, columns], preferred_element_type=jnp.float32
            ).astype(jnp.bfloat16)

        low_q = lax.broadcasted_iota(jnp.int32, (PAD, 128), 1) < HEAD_DIM
        low_k = lax.broadcasted_iota(jnp.int32, (KEYS, 128), 1) < HEAD_DIM
        real = lax.broadcasted_iota(jnp.int32, (PAD, 128), 1) == 0
        zero = jnp.zeros((), jnp.bfloat16)
        one = jnp.ones((), jnp.bfloat16)
        for pair in range(HEADS // 2):
            lanes = slice(128 * pair, 128 * pair + 128)
            queries = qkv_rows[:PAD, lanes]
            keys = qkv_rows[:, D + 128 * pair : D + 128 * pair + 128]
            values = qkv_rows[:, 2 * D + 128 * pair : 2 * D + 128 * pair + 128]
            sums = []
            for low in (True, False):
                here_q = low_q if low else jnp.logical_not(low_q)
                here_k = low_k if low else jnp.logical_not(low_k)
                scores = lax.dot_general(
                    jnp.where(here_q, queries, zero),
                    keys,
                    (((1,), (1,)), ((), ())),
                    preferred_element_type=jnp.float32,
                )
                main, last = scores[:, :256], jnp.where(real, scores[:, 256:], -1e30)
                row_max = jnp.maximum(
                    jnp.max(main, axis=-1, keepdims=True), jnp.max(last, axis=-1, keepdims=True)
                )
                factor = HEAD_DIM ** (-0.5) * math.log2(math.e)
                powered = jnp.concatenate(
                    [jnp.exp2((main - row_max) * factor), jnp.exp2((last - row_max) * factor)], axis=1
                ).astype(jnp.bfloat16)
                sums.append(
                    jnp.dot(powered, jnp.where(here_k, values, one), preferred_element_type=jnp.float32)
                )
            own = jnp.where(low_q, sums[0], sums[1])
            total = pltpu.roll(jnp.where(low_q, sums[1], sums[0]), HEAD_DIM, 1)
            context[:, lanes] = (own / total).astype(jnp.bfloat16)

        projected = jnp.dot(context[:SEQ], w_out[...], preferred_element_type=jnp.float32)
        out_ref[image] = (block_in[...].astype(jnp.float32) + projected).astype(jnp.bfloat16)

    if images == 1:
        one_image(0)
    else:
        pl.loop(0, images)(one_image)


def run_block(first_image, images, pieces, place, streams, skips, sides, times, gain_row, mine, other):
    whole = pl.BlockSpec(memory_space=pltpu.VMEM)
    there = pl.BlockSpec(memory_space=pl.ANY)

    def body(*refs):
        block_kernel(images, first_image, pieces, *refs)

    return pl.pallas_call(
        body,
        out_shape=jax.ShapeDtypeStruct((images, SEQ, D), jnp.bfloat16),
        in_specs=[pl.BlockSpec(memory_space=pltpu.SMEM), whole, whole, there, there]
        + [whole] * (3 * len(pieces)),
        out_specs=whole,
        scratch_shapes=[
            pltpu.VMEM((D, 3 * D), jnp.bfloat16),
            pltpu.VMEM((D, D), jnp.bfloat16),
            pltpu.VMEM((2 * D, D), jnp.bfloat16),
            pltpu.VMEM((images, SEQ, D), jnp.bfloat16),
            pltpu.VMEM((images, SEQ, D), jnp.bfloat16),
            pltpu.VMEM((SEQ, D), jnp.bfloat16),
            pltpu.VMEM((KEYS, 3 * D), jnp.bfloat16),
            pltpu.VMEM((PAD, D), jnp.bfloat16),
            pltpu.SemaphoreType.DMA((40,)),
        ],
        compiler_params=pltpu.CompilerParams(vmem_limit_bytes=40 * 2**20),
        cost_estimate=pl.CostEstimate(
            flops=images * 2 * SEQ * D * D * 7, bytes_accessed=8 * 2**20, transcendentals=0
        ),
    )(place, times, gain_row, mine, other, *streams, *skips, *sides)


def on_device(
    stream_in, timestep, ln_gain, qkv_weight, out_weight, join_weight, ctx_saved, out_cot
):
    section = lax.axis_index(SECTION)
    core = lax.axis_index("c")
    y_low = lax.axis_index("yl")
    place = jnp.stack([core, section]).astype(jnp.int32)
    onward = [(s, (s + 1) % SECTIONS) for s in range(SECTIONS)]
    swap = [(0, 1), (1, 0)]

    term = lax.dot_general(
        ctx_saved[0], out_cot[0], (((0,), (0,)), ((), ())), preferred_element_type=jnp.float32
    )
    left, right = term[:, : D // 2], term[:, D // 2 :]
    chip = jnp.where(core == 0, left, right) + lax.ppermute(
        jnp.where(core == 0, right, left), "c", swap
    )
    level = lax.psum_scatter(chip, "z", scatter_dimension=0, tiled=True)

    join_rows = lax.dynamic_index_in_dim(
        join_weight, jnp.clip(section - 4, 0, 3), 0, keepdims=False
    )
    for_low = qkv_weight[0].reshape(12, 3, D).transpose(1, 0, 2).reshape(36, D)
    for_high = jnp.concatenate([out_weight[0], join_rows], axis=0)
    straight = lax.ppermute(jnp.where(core == 0, for_low, for_high), SECTION, onward)
    crossed = lax.ppermute(
        jnp.where(core == 0, for_high, for_low),
        AXES,
        [
            (i, ((i // REPLICAS + 1) % SECTIONS) * REPLICAS + ((i % REPLICAS) ^ 1))
            for i in range(SECTIONS * REPLICAS)
        ],
    )
    pair = jnp.where(
        core == 0,
        jnp.concatenate([straight, crossed], axis=0),
        jnp.concatenate([crossed, straight], axis=0),
    )
    near = lax.all_gather(pair, "yl", axis=0, tiled=True)
    slot = lax.broadcasted_iota(jnp.int32, (288, 288), 0)
    source = lax.broadcasted_iota(jnp.int32, (288, 288), 1)
    from_qkv = (slot % 96) // 12 * 36 + slot // 96 * 12 + slot % 12
    rest = slot - 96
    from_rest = jnp.where(slot < 96, slot // 12 * 36 + slot % 12, rest // 24 * 36 + 12 + rest % 24)
    order = (source == jnp.where(core == 0, from_qkv, from_rest)).astype(jnp.bfloat16)
    near = jnp.dot(order, near, preferred_element_type=jnp.float32).astype(jnp.bfloat16)

    def onwards(part):
        return lax.ppermute(part, SECTION, onward), lax.ppermute(part, SECTION, [(1, 0), (2, 7)])

    def beside(part):
        return lax.ppermute(part, SECTION, [(3, 5)])

    def beside_on(part):
        return lax.ppermute(part, SECTION, [(5, 6)])

    image_0, image_1 = stream_in[0, :SEQ], stream_in[0, SEQ : 2 * SEQ]
    image_2 = stream_in[0, 2 * SEQ :]
    gain_row = lax.ppermute(ln_gain, SECTION, onward)
    stream_0, skip_0 = onwards(image_0)
    side_0 = beside_on(beside(image_0))
    side_1, side_2 = beside(image_1), beside(image_2)

    near, level, gain_row, stream_0, skip_0, side_0, side_1, side_2, image_1, image_2 = (
        lax.optimization_barrier(
            (near, level, gain_row, stream_0, skip_0, side_0, side_1, side_2, image_1, image_2)
        )
    )
    mine = lax.all_gather(near, "z", axis=0, tiled=False)
    stream_1, skip_1 = onwards(image_1)
    stream_2, skip_2 = onwards(image_2[:CUT])
    side_1, side_2 = beside_on(side_1), beside_on(side_2)

    level = level.reshape(4, 24, D // 2)
    total = lax.dynamic_index_in_dim(level, y_low, 0, keepdims=False)
    for step in range(1, 4):
        ring = [(i, (i + step) % 4) for i in range(4)]
        piece = lax.dynamic_index_in_dim(level, (y_low + step) % 4, 0, keepdims=False)
        total = total + lax.ppermute(piece, "yl", ring)
    low_rows, high_rows = total[:12], total[12:]
    own_half = jnp.where(core == 0, low_rows, high_rows)
    other_half = lax.ppermute(jnp.where(core == 0, high_rows, low_rows), "c", swap)
    weight_grad = jnp.where(
        core == 0,
        jnp.concatenate([own_half, other_half], axis=1),
        jnp.concatenate([other_half, own_half], axis=1),
    )

    (
        mine,
        weight_grad,
        stream_1,
        skip_1,
        side_1,
        stream_2,
        skip_2,
        side_2,
        image_2,
    ) = lax.optimization_barrier(
        (mine, weight_grad, stream_1, skip_1, side_1, stream_2, skip_2, side_2, image_2)
    )
    other = lax.ppermute(mine, "c", swap)
    stream_3, skip_3 = onwards(image_2[CUT:])

    times = time_rows(timestep).astype(jnp.float32).reshape(-1, 1, D)
    front_out = run_block(
        0,
        2,
        ((0, 0, SEQ), (1, 0, SEQ)),
        place,
        (stream_0, stream_1),
        (skip_0, skip_1),
        (side_0, side_1),
        times,
        gain_row,
        mine,
        other,
    )
    back_out = run_block(
        2,
        1,
        ((0, 0, CUT), (0, CUT, SEQ - CUT)),
        place,
        (stream_2, stream_3),
        (skip_2, skip_3),
        (side_2[:CUT], side_2[CUT:]),
        times,
        gain_row,
        mine,
        other,
    )
    stream_out = jnp.concatenate(
        [front_out.reshape(2 * SEQ, D), back_out.reshape(SEQ, D)], axis=0
    )
    return (stream_out[None], weight_grad[None])


def solution(mesh):
    fine = Mesh(mesh.devices.reshape(4, 2, 8, 4, 2), AXES)
    section, dp = ("x", "yh"), ("z", "yl", "c")
    return jax.shard_map(
        on_device,
        mesh=fine,
        in_specs=(
            P(section, dp, None),
            P(dp),
            P(section, None),
            P(section, dp, None),
            P(section, dp, None),
            P(None, dp, None),
            P(section, dp, None),
            P(section, dp, None),
        ),
        out_specs=(P(section, dp, None), P(section, dp, None)),
        check_vma=False,
    )
```

time: 700 us -> 233 us (0.33)
  the two profiles are of different devices: /device:TPU:1 before, /device:TPU:373 now
where the time goes in v1:
time: 233 us; the launch traced here: 232 us
  starting transfers between devices  101 us (43%)
  waiting for transfers between devices  36.5 us (16%)
  blocking collectives  27.2 us (12%)
  Pallas kernels  22.2 us (10%)
  local copies, waits for them, and re-layouts  21.2 us (9%)
  between operations  14.7 us (6%)
  matrix products  5.43 us (2%)
  other arithmetic  3.63 us (2%)
    ppermute x1, starting transfers between devices, on_device(): lax.ppermute(jnp.where(core == 0, high_rows, low_rows), 'c', swap)  39.5 us
    all_gather x1, blocking collectives, on_device(): near = lax.all_gather(pair, 'yl', axis=0, tiled=True)  27.2 us
    pallas_call x2, Pallas kernels, run_block(): pl.pallas_call(body, out_shape=jax.ShapeDtypeStruct((images, SEQ, D), jnp...  22.2 us
    ppermute x4, waiting for transfers between devices, onwards(): lax.ppermute(part, SECTION, onward)  17.8 us
    ppermute x4, starting transfers between devices, onwards(): lax.ppermute(part, SECTION, onward)  16.9 us
    unnamed x46, local copies, waits for them, and re-layouts  14.7 us
    ppermute x1, waiting for transfers between devices, on_device(): lax.ppermute(jnp.where(core == 0, for_high, for_low), AXES, [(i, (i // RE...  12.8 us
    ppermute x3, starting transfers between devices, on_device(): total = total + lax.ppermute(piece, 'yl', ring)  8.97 us
  transfers between devices with their start and end apart: 25, of which 5 were waited for; matrix products, arithmetic and copies ran while one was open for 4% of the time, Pallas kernels for 6%

profile of v1, /device:TPU:373, one launch (start us, length us, event | category | flops | bytes accessed | tf_op | source)
XLA Modules:
  0.0 232.1 jit_solution(669255278246386224)
XLA Ops:
  8.4 2.7 %fusion = f32[768,768]{1,0:T(8,128)S(1)} fusion(bf16[1,771,768]{2,1,0:T(8,128)(2,1)S(1)} %copy-done, bf16[1,771,768]{2,1,0:T(8,128)(2,1)} %param.14), kind=kOutput, calls=%fused_computation.2 | convolution fusion | flops 909508608 | bytes 4727808 | tf_op jit(solution)/shard_map/dot_general | solution.py:202
  11.3 2.6 %collective-permute-start.2 = (f32[768,384]{1,0:T(8,128)S(1)}, f32[768,384]{1,0:T(8,128)S(1)}, u32[]{:S(2)}, u32[]{:S(2)}) collective-permute-start(f32[768,384]{1,0:T(8,128)S(1)} %slice_select_fusion), channel_id=1, source_target_pairs={{0,1},{1,0},{2,3},{3,2},{4,5},{5,4},{6,7},{7,6},{8,9},{9,8},{10,11... | collective-permute-start | bytes 3538952 | tf_op jit(solution)/shard_map/ppermute | solution.py:206
  13.9 2.5 %collective-permute-done.2 = f32[768,384]{1,0:T(8,128)S(1)} collective-permute-done((f32[768,384]{1,0:T(8,128)S(1)}, f32[768,384]{1,0:T(8,128)S(1)}, u32[]{:S(2)}, u32[]{:S(2)}) %collective-permute-start.2) | collective-permute-done | bytes 1179680 | tf_op jit(solution)/shard_map/ppermute | solution.py:206
  19.2 4.2 %collective-permute-start.4 = (bf16[257,768]{1,0:T(8,128)(2,1)}, bf16[257,768]{1,0:T(8,128)(2,1)S(1)}, u32[]{:S(2)}, u32[]{:S(2)}) collective-permute-start(bf16[257,768]{1,0:T(8,128)(2,1)} %get-tuple-element.41), channel_id=1, source_target_pairs={{0,64},{64,128},{128,192},{192,256},{256,320},{320,384},{384,448},... | collective-permute-start | bytes 1184264 | tf_op jit(solution)/shard_map/ppermute | solution.py:240
  24.0 1.3 collective-permute-start.6
  26.2 6.3 %collective-permute-start.1 = (bf16[36,768]{1,0:T(8,128)(2,1)S(1)}, bf16[36,768]{1,0:T(8,128)(2,1)S(1)}, u32[]{:S(2)}, u32[]{:S(2)}) collective-permute-start(bf16[36,768]{1,0:T(8,128)(2,1)S(1)} %get-tuple-element.47), channel_id=1, source_target_pairs={{0,65},{1,64},{2,67},{3,66},{4,69},{5,68},{6,71},{7,70},{8,73},{9,... | collective-permute-start | bytes 165896 | tf_op jit(solution)/shard_map/ppermute | solution.py:217
  32.6 4.1 %collective-permute-start = (bf16[36,768]{1,0:T(8,128)(2,1)S(1)}, bf16[36,768]{1,0:T(8,128)(2,1)S(1)}, u32[]{:S(2)}, u32[]{:S(2)}) collective-permute-start(bf16[36,768]{1,0:T(8,128)(2,1)S(1)} %get-tuple-element.46), channel_id=1, source_target_pairs={{0,64},{64,128},{128,192},{192,256},{256,320},{320,384},{384,448},... | collective-permute-start | bytes 165896 | tf_op jit(solution)/shard_map/ppermute | solution.py:216
  36.8 12.8 %collective-permute-done.1 = bf16[36,768]{1,0:T(8,128)(2,1)S(1)} collective-permute-done((bf16[36,768]{1,0:T(8,128)(2,1)S(1)}, bf16[36,768]{1,0:T(8,128)(2,1)S(1)}, u32[]{:S(2)}, u32[]{:S(2)}) %collective-permute-start.1) | collective-permute-done | bytes 55328 | tf_op jit(solution)/shard_map/ppermute | solution.py:217
  49.6 4.4 %collective-permute-start.3 = (f32[1,768]{1,0:T(1,128)S(1)}, f32[1,768]{1,0:T(1,128)S(1)}, u32[]{:S(2)}, u32[]{:S(2)}) collective-permute-start(f32[1,768]{1,0:T(1,128)S(1)} %copy-done.21), channel_id=1, source_target_pairs={{0,64},{64,128},{128,192},{192,256},{256,320},{320,384},{384,448},... | collective-permute-start | bytes 9224 | tf_op jit(solution)/shard_map/ppermute | solution.py:250
  54.0 1.3 collective-permute-start.8
  55.3 2.5 %collective-permute-done.3.refs_2_ = f32[1,768]{1,0:T(1,128)S(1)} collective-permute-done((f32[1,768]{1,0:T(1,128)S(1)}, f32[1,768]{1,0:T(1,128)S(1)}, u32[]{:S(2)}, u32[]{:S(2)}) %collective-permute-start.3) | collective-permute-done | bytes 3104 | tf_op jit(solution)/shard_map/ppermute | solution.py:250
  57.8 1.3 collective-permute-start.9
  59.1 5.4 %collective-permute-start.7 = (bf16[257,768]{1,0:T(8,128)(2,1)}, bf16[257,768]{1,0:T(8,128)(2,1)S(1)}, u32[]{:S(2)}, u32[]{:S(2)}) collective-permute-start(bf16[257,768]{1,0:T(8,128)(2,1)} %collective-permute-done.6), channel_id=1, source_target_pairs={{320,384},{321,385},{322,386},{323,387},{324,388},{325,389},{326,3... | collective-permute-start | bytes 1184264 | tf_op jit(solution)/shard_map/ppermute | solution.py:246
  64.5 27.2 %all_gather.9 = bf16[288,768]{1,0:T(8,128)(2,1)S(1)} all-gather(bf16[72,768]{1,0:T(8,128)(2,1)S(1)} %maximum_select_fusion), channel_id=1, replica_groups=mesh['x'=4,'yh'=2,'z'=8,'yl'=4,'c'=2] {'yl'}, dimensions={0}, use_global_device_ids=true | all-gather | bytes 552960 | tf_op jit(solution)/shard_map/all_gather | solution.py:230
  91.8 2.7 %convolution_convert_fusion = bf16[288,768]{1,0:T(8,128)(2,1)} fusion(bf16[288,768]{1,0:T(8,128)(2,1)S(1)} %all_gather.9, s32[288]{0:T(512)S(1)} %get-tuple-element.63, s32[288]{0:T(512)S(1)} %get-tuple-element.66, s32[288]{0:T(512)S(1)} %get-tuple-element.62, s32[288]{0:T(512)S(1)} %get-tuple-element.67, s32[288]{0:T(512)S(1)} %get-tuple-element.61, ...), kind=kOutput, calls=%fused_computation | convolution fusion | flops 129779712 | bytes 900577 | tf_op jit(solution)/shard_map/dot_general | solution.py:237
  95.6 1.9 collective-permute-start.12
  97.5 4.7 %collective-permute-start.11 = (f32[24,384]{1,0:T(8,128)S(1)}, f32[24,384]{1,0:T(8,128)S(1)}, u32[]{:S(2)}, u32[]{:S(2)}) collective-permute-start(f32[24,384]{1,0:T(8,128)S(1)} %get-tuple-element.45), channel_id=1, source_target_pairs={{0,4},{2,6},{4,0},{6,2},{1,5},{3,7},{5,1},{7,3},{8,12},{10,14},{12... | collective-permute-start | bytes 110600 | tf_op jit(solution)/shard_map/ppermute | solution.py:270
  102.2 2.4 %collective-permute-start.10 = (f32[24,384]{1,0:T(8,128)S(1)}, f32[24,384]{1,0:T(8,128)S(1)}, u32[]{:S(2)}, u32[]{:S(2)}) collective-permute-start(f32[24,384]{1,0:T(8,128)S(1)} %get-tuple-element.43), channel_id=1, source_target_pairs={{0,2},{2,4},{4,6},{6,0},{1,3},{3,5},{5,7},{7,1},{8,10},{10,12},{12... | collective-permute-start | bytes 110600 | tf_op jit(solution)/shard_map/ppermute | solution.py:270
  104.6 1.9 collective-permute-start.14
  107.2 1.3 collective-permute-start.16
  108.5 2.0 collective-permute-start.19
  111.4 39.5 %collective-permute-start.13 = (f32[12,384]{1,0:T(8,128)S(1)}, f32[12,384]{1,0:T(8,128)S(1)}, u32[]{:S(2)}, u32[]{:S(2)}) collective-permute-start(f32[12,384]{1,0:T(8,128)S(1)} %get-tuple-element.49), channel_id=1, source_target_pairs={{0,1},{1,0},{2,3},{3,2},{4,5},{5,4},{6,7},{7,6},{8,9},{9,8},{10,11... | collective-permute-start | bytes 55304 | tf_op jit(solution)/shard_map/ppermute | solution.py:273
  151.7 1.9 collective-permute-start.17
  153.6 17.8 %collective-permute-done.17.refs_5_ = bf16[112,768]{1,0:T(8,128)(2,1)S(1)} collective-permute-done((bf16[112,768]{1,0:T(8,128)(2,1)S(1)}, bf16[112,768]{1,0:T(8,128)(2,1)S(1)}, u32[]{:S(2)}, u32[]{:S(2)}) %collective-permute-start.17) | collective-permute-done | bytes 172064 | tf_op jit(solution)/shard_map/ppermute | solution.py:240
  174.4 3.1 %collective-permute-start.20 = (bf16[8,288,768]{2,1,0:T(8,128)(2,1)}, bf16[8,288,768]{2,1,0:T(8,128)(2,1)S(1)}, u32[]{:S(2)}, u32[]{:S(2)}) collective-permute-start(bf16[8,288,768]{2,1,0:T(8,128)(2,1)} %bitcast.40), channel_id=1, source_target_pairs={{0,1},{1,0},{2,3},{3,2},{4,5},{5,4},{6,7},{7,6},{8,9},{9,8},{10,11... | collective-permute-start | bytes 10616840 | tf_op jit(solution)/shard_map/ppermute | solution.py:293
  177.9 9.0 %collective-permute-start.21 = (bf16[145,768]{1,0:T(8,128)(2,1)S(1)}, bf16[145,768]{1,0:T(8,128)(2,1)S(1)}, u32[]{:S(2)}, u32[]{:S(2)}) collective-permute-start(bf16[145,768]{1,0:T(8,128)(2,1)S(1)} %slice.41), channel_id=1, source_target_pairs={{0,64},{64,128},{128,192},{192,256},{256,320},{320,384},{384,448},... | collective-permute-start | bytes 668168 | tf_op jit(solution)/shard_map/ppermute | solution.py:240
  190.1 2.0 copy-done.1
  195.1 13.5 %shard_map.95 = bf16[2,257,768]{2,1,0:T(8,128)(2,1)S(1)} custom-call(s32[2]{0:T(128)S(1)} %pad_add_fusion.refs_0_, f32[3,1,768]{2,1,0:T(1,128)S(1)} %maximum_convert_fusion.refs_1_, f32[1,768]{1,0:T(1,128)S(1)} %collective-permute-done.3.refs_2_, bf16[8,288,768]{2,1,0:T(8,128)(2,1)S(1)} %bitcast.41, ...), custom_call_target="tpu_custom_call" | custom-call | flops 4244373504 | bytes 8388608 | tf_op jit(solution)/shard_map/pallas_call | solution.py:168
  208.7 1.7 copy-done.3
  211.5 2.0 copy-done.2
  213.5 2.0 copy-done.4
  215.5 8.6 %shard_map.96 = bf16[1,257,768]{2,1,0:T(8,128)(2,1)S(1)} custom-call(s32[2]{0:T(128)S(1)} %pad_add_fusion.refs_0_, f32[3,1,768]{2,1,0:T(1,128)S(1)} %maximum_convert_fusion.refs_1_, f32[1,768]{1,0:T(1,128)S(1)} %collective-permute-done.3.refs_2_, bf16[8,288,768]{2,1,0:T(8,128)(2,1)S(1)} %bitcast.42, bf16[8,288,768]{2,1,0:T(8,128)(2,1)S(1)} %copy-done.4, ...), custom_call_target="tpu_custom_call" | custom-call | flops 2122186752 | bytes 8388608 | tf_op jit(solution)/shard_map/pallas_call | solution.py:168
  (108 shorter events, 20.8 us)
Async XLA Ops:
  7.2 87.4 %reduce-scatter.2.cloned.1.call-start = ((), (), s32[]{:S(2)}) async-start(), calls=%async_computation.1 | async-start | bytes 1327104 | tf_op jit(solution)/shard_map/reduce_scatter | solution.py:209
  11.3 5.0 %collective-permute-start.2 = (f32[768,384]{1,0:T(8,128)S(1)}, f32[768,384]{1,0:T(8,128)S(1)}, u32[]{:S(2)}, u32[]{:S(2)}) collective-permute-start(f32[768,384]{1,0:T(8,128)S(1)} %slice_select_fusion), channel_id=1, source_target_pairs={{0,1},{1,0},{2,3},{3,2},{4,5},{5,4},{6,7},{7,6},{8,9},{9,8},{10,11... | collective-permute-start | bytes 3538952 | tf_op jit(solution)/shard_map/ppermute | solution.py:206
  17.6 32.0 %copy-start.21 = (f32[1,768]{1,0:T(1,128)S(1)}, f32[1,768]{1,0:T(1,128)}, u32[]{:S(2)}) copy-start(f32[1,768]{1,0:T(1,128)} %param.10) | copy-start | bytes 9220
  17.6 156.8 %all-gather.3.cloned.1.call-start = ((), (), s32[]{:S(2)}) async-start(), calls=%async_computation.2 | async-start | bytes 3981312 | tf_op jit(solution)/shard_map/all_gather | solution.py:260
  19.2 75.3 %collective-permute-start.4 = (bf16[257,768]{1,0:T(8,128)(2,1)}, bf16[257,768]{1,0:T(8,128)(2,1)S(1)}, u32[]{:S(2)}, u32[]{:S(2)}) collective-permute-start(bf16[257,768]{1,0:T(8,128)(2,1)} %get-tuple-element.41), channel_id=1, source_target_pairs={{0,64},{64,128},{128,192},{192,256},{256,320},{320,384},{384,448},... | collective-permute-start | bytes 1184264 | tf_op jit(solution)/shard_map/ppermute | solution.py:240
  23.3 71.2 %collective-permute-start.5 = (bf16[257,768]{1,0:T(8,128)(2,1)}, bf16[257,768]{1,0:T(8,128)(2,1)S(1)}, u32[]{:S(2)}, u32[]{:S(2)}) collective-permute-start(bf16[257,768]{1,0:T(8,128)(2,1)} %get-tuple-element.41), channel_id=1, source_target_pairs={{64,0},{128,448},{65,1},{129,449},{66,2},{130,450},{67,3},{131,451... | collective-permute-start | bytes 1184264 | tf_op jit(solution)/shard_map/ppermute | solution.py:240
  24.0 35.1 %collective-permute-start.6 = (bf16[257,768]{1,0:T(8,128)(2,1)}, bf16[257,768]{1,0:T(8,128)(2,1)}, u32[]{:S(2)}, u32[]{:S(2)}) collective-permute-start(bf16[257,768]{1,0:T(8,128)(2,1)} %get-tuple-element.41), channel_id=1, source_target_pairs={{192,320},{193,321},{194,322},{195,323},{196,324},{197,325},{198,3... | collective-permute-start | bytes 1184264 | tf_op jit(solution)/shard_map/ppermute | solution.py:243
  26.2 23.3 %collective-permute-start.1 = (bf16[36,768]{1,0:T(8,128)(2,1)S(1)}, bf16[36,768]{1,0:T(8,128)(2,1)S(1)}, u32[]{:S(2)}, u32[]{:S(2)}) collective-permute-start(bf16[36,768]{1,0:T(8,128)(2,1)S(1)} %get-tuple-element.47), channel_id=1, source_target_pairs={{0,65},{1,64},{2,67},{3,66},{4,69},{5,68},{6,71},{7,70},{8,73},{9,... | collective-permute-start | bytes 165896 | tf_op jit(solution)/shard_map/ppermute | solution.py:217
  32.6 21.4 %collective-permute-start = (bf16[36,768]{1,0:T(8,128)(2,1)S(1)}, bf16[36,768]{1,0:T(8,128)(2,1)S(1)}, u32[]{:S(2)}, u32[]{:S(2)}) collective-permute-start(bf16[36,768]{1,0:T(8,128)(2,1)S(1)} %get-tuple-element.46), channel_id=1, source_target_pairs={{0,64},{64,128},{128,192},{192,256},{256,320},{320,384},{384,448},... | collective-permute-start | bytes 165896 | tf_op jit(solution)/shard_map/ppermute | solution.py:216
  49.6 8.2 %collective-permute-start.3 = (f32[1,768]{1,0:T(1,128)S(1)}, f32[1,768]{1,0:T(1,128)S(1)}, u32[]{:S(2)}, u32[]{:S(2)}) collective-permute-start(f32[1,768]{1,0:T(1,128)S(1)} %copy-done.21), channel_id=1, source_target_pairs={{0,64},{64,128},{128,192},{192,256},{256,320},{320,384},{384,448},... | collective-permute-start | bytes 9224 | tf_op jit(solution)/shard_map/ppermute | solution.py:250
  54.0 40.5 %collective-permute-start.8 = (bf16[257,768]{1,0:T(8,128)(2,1)}, bf16[257,768]{1,0:T(8,128)(2,1)}, u32[]{:S(2)}, u32[]{:S(2)}) collective-permute-start(bf16[257,768]{1,0:T(8,128)(2,1)} %get-tuple-element.24), channel_id=1, source_target_pairs={{192,320},{193,321},{194,322},{195,323},{196,324},{197,325},{198,3... | collective-permute-start | bytes 1184264 | tf_op jit(solution)/shard_map/ppermute | solution.py:243
  57.8 36.7 %collective-permute-start.9 = (bf16[257,768]{1,0:T(8,128)(2,1)S(1)}, bf16[257,768]{1,0:T(8,128)(2,1)}, u32[]{:S(2)}, u32[]{:S(2)}) collective-permute-start(bf16[257,768]{1,0:T(8,128)(2,1)S(1)} %get-tuple-element.36), channel_id=1, source_target_pairs={{192,320},{193,321},{194,322},{195,323},{196,324},{197,325},{198,3... | collective-permute-start | bytes 1184264 | tf_op jit(solution)/shard_map/ppermute | solution.py:243
  59.1 35.4 %collective-permute-start.7 = (bf16[257,768]{1,0:T(8,128)(2,1)}, bf16[257,768]{1,0:T(8,128)(2,1)S(1)}, u32[]{:S(2)}, u32[]{:S(2)}) collective-permute-start(bf16[257,768]{1,0:T(8,128)(2,1)} %collective-permute-done.6), channel_id=1, source_target_pairs={{320,384},{321,385},{322,386},{323,387},{324,388},{325,389},{326,3... | collective-permute-start | bytes 1184264 | tf_op jit(solution)/shard_map/ppermute | solution.py:246
  94.5 83.1 %copy-start.22 = (s32[3]{0:T(128)S(1)}, s32[3]{0:T(128)}, u32[]{:S(2)}) copy-start(s32[3]{0:T(128)} %param.9) | copy-start | bytes 40
  94.5 93.1 %copy-start.5 = (bf16[257,768]{1,0:T(8,128)(2,1)}, bf16[257,768]{1,0:T(8,128)(2,1)S(1)}, u32[]{:S(2)}) copy-start(bf16[257,768]{1,0:T(8,128)(2,1)S(1)} %collective-permute-done.4.refs_5_) | copy-start | bytes 1184260
  94.5 95.0 %copy-start.7 = (bf16[257,768]{1,0:T(8,128)(2,1)}, bf16[257,768]{1,0:T(8,128)(2,1)S(1)}, u32[]{:S(2)}) copy-start(bf16[257,768]{1,0:T(8,128)(2,1)S(1)} %collective-permute-done.5.refs_7_) | copy-start | bytes 1184260
  94.5 92.3 %copy-start.9 = (bf16[257,768]{1,0:T(8,128)(2,1)}, bf16[257,768]{1,0:T(8,128)(2,1)S(1)}, u32[]{:S(2)}) copy-start(bf16[257,768]{1,0:T(8,128)(2,1)S(1)} %collective-permute-done.7.refs_9_) | copy-start | bytes 1184260
  95.6 11.6 %collective-permute-start.12 = (f32[24,384]{1,0:T(8,128)S(1)}, f32[24,384]{1,0:T(8,128)S(1)}, u32[]{:S(2)}, u32[]{:S(2)}) collective-permute-start(f32[24,384]{1,0:T(8,128)S(1)} %get-tuple-element.44), channel_id=1, source_target_pairs={{0,6},{2,0},{4,2},{6,4},{1,7},{3,1},{5,3},{7,5},{8,14},{10,8},{12,... | collective-permute-start | bytes 110600 | tf_op jit(solution)/shard_map/ppermute | solution.py:270
  97.5 11.0 %collective-permute-start.11 = (f32[24,384]{1,0:T(8,128)S(1)}, f32[24,384]{1,0:T(8,128)S(1)}, u32[]{:S(2)}, u32[]{:S(2)}) collective-permute-start(f32[24,384]{1,0:T(8,128)S(1)} %get-tuple-element.45), channel_id=1, source_target_pairs={{0,4},{2,6},{4,0},{6,2},{1,5},{3,7},{5,1},{7,3},{8,12},{10,14},{12... | collective-permute-start | bytes 110600 | tf_op jit(solution)/shard_map/ppermute | solution.py:270
  102.2 8.4 %collective-permute-start.10 = (f32[24,384]{1,0:T(8,128)S(1)}, f32[24,384]{1,0:T(8,128)S(1)}, u32[]{:S(2)}, u32[]{:S(2)}) collective-permute-start(f32[24,384]{1,0:T(8,128)S(1)} %get-tuple-element.43), channel_id=1, source_target_pairs={{0,2},{2,4},{4,6},{6,0},{1,3},{3,5},{5,7},{7,1},{8,10},{10,12},{12... | collective-permute-start | bytes 110600 | tf_op jit(solution)/shard_map/ppermute | solution.py:270
  104.6 67.5 %collective-permute-start.14 = (bf16[257,768]{1,0:T(8,128)(2,1)}, bf16[257,768]{1,0:T(8,128)(2,1)S(1)}, u32[]{:S(2)}, u32[]{:S(2)}) collective-permute-start(bf16[257,768]{1,0:T(8,128)(2,1)} %get-tuple-element.24), channel_id=1, source_target_pairs={{0,64},{64,128},{128,192},{192,256},{256,320},{320,384},{384,448},... | collective-permute-start | bytes 1184264 | tf_op jit(solution)/shard_map/ppermute | solution.py:240
  106.5 66.4 %collective-permute-start.15 = (bf16[257,768]{1,0:T(8,128)(2,1)}, bf16[257,768]{1,0:T(8,128)(2,1)S(1)}, u32[]{:S(2)}, u32[]{:S(2)}) collective-permute-start(bf16[257,768]{1,0:T(8,128)(2,1)} %get-tuple-element.24), channel_id=1, source_target_pairs={{64,0},{128,448},{65,1},{129,449},{66,2},{130,450},{67,3},{131,451... | collective-permute-start | bytes 1184264 | tf_op jit(solution)/shard_map/ppermute | solution.py:240
  107.2 66.4 %collective-permute-start.16 = (bf16[257,768]{1,0:T(8,128)(2,1)}, bf16[257,768]{1,0:T(8,128)(2,1)S(1)}, u32[]{:S(2)}, u32[]{:S(2)}) collective-permute-start(bf16[257,768]{1,0:T(8,128)(2,1)} %collective-permute-done.8), channel_id=1, source_target_pairs={{320,384},{321,385},{322,386},{323,387},{324,388},{325,389},{326,3... | collective-permute-start | bytes 1184264 | tf_op jit(solution)/shard_map/ppermute | solution.py:246
  108.5 65.9 %collective-permute-start.19 = (bf16[257,768]{1,0:T(8,128)(2,1)}, bf16[257,768]{1,0:T(8,128)(2,1)}, u32[]{:S(2)}, u32[]{:S(2)}) collective-permute-start(bf16[257,768]{1,0:T(8,128)(2,1)} %collective-permute-done.9), channel_id=1, source_target_pairs={{320,384},{321,385},{322,386},{323,387},{324,388},{325,389},{326,3... | collective-permute-start | bytes 1184264 | tf_op jit(solution)/shard_map/ppermute | solution.py:246
  111.4 40.3 %collective-permute-start.13 = (f32[12,384]{1,0:T(8,128)S(1)}, f32[12,384]{1,0:T(8,128)S(1)}, u32[]{:S(2)}, u32[]{:S(2)}) collective-permute-start(f32[12,384]{1,0:T(8,128)S(1)} %get-tuple-element.49), channel_id=1, source_target_pairs={{0,1},{1,0},{2,3},{3,2},{4,5},{5,4},{6,7},{7,6},{8,9},{9,8},{10,11... | collective-permute-start | bytes 55304 | tf_op jit(solution)/shard_map/ppermute | solution.py:273
  151.7 19.7 %collective-permute-start.17 = (bf16[112,768]{1,0:T(8,128)(2,1)S(1)}, bf16[112,768]{1,0:T(8,128)(2,1)S(1)}, u32[]{:S(2)}, u32[]{:S(2)}) collective-permute-start(bf16[112,768]{1,0:T(8,128)(2,1)S(1)} %slice.40), channel_id=1, source_target_pairs={{0,64},{64,128},{128,192},{192,256},{256,320},{320,384},{384,448},... | collective-permute-start | bytes 516104 | tf_op jit(solution)/shard_map/ppermute | solution.py:240
  171.4 0.7 collective-permute-start.18
  174.4 15.7 %copy-start.14 = (bf16[257,768]{1,0:T(8,128)(2,1)S(1)}, bf16[257,768]{1,0:T(8,128)(2,1)}, u32[]{:S(2)}) copy-start(bf16[257,768]{1,0:T(8,128)(2,1)} %copy-done.13) | copy-start | bytes 1184260
  174.4 15.7 %copy-start.16 = (bf16[257,768]{1,0:T(8,128)(2,1)S(1)}, bf16[257,768]{1,0:T(8,128)(2,1)}, u32[]{:S(2)}) copy-start(bf16[257,768]{1,0:T(8,128)(2,1)} %copy-done.15) | copy-start | bytes 1184260
  174.4 15.7 %collective-permute-start.20 = (bf16[8,288,768]{2,1,0:T(8,128)(2,1)}, bf16[8,288,768]{2,1,0:T(8,128)(2,1)S(1)}, u32[]{:S(2)}, u32[]{:S(2)}) collective-permute-start(bf16[8,288,768]{2,1,0:T(8,128)(2,1)} %bitcast.40), channel_id=1, source_target_pairs={{0,1},{1,0},{2,3},{3,2},{4,5},{5,4},{6,7},{7,6},{8,9},{9,8},{10,11... | collective-permute-start | bytes 10616840 | tf_op jit(solution)/shard_map/ppermute | solution.py:293
  177.9 33.6 %collective-permute-start.21 = (bf16[145,768]{1,0:T(8,128)(2,1)S(1)}, bf16[145,768]{1,0:T(8,128)(2,1)S(1)}, u32[]{:S(2)}, u32[]{:S(2)}) collective-permute-start(bf16[145,768]{1,0:T(8,128)(2,1)S(1)} %slice.41), channel_id=1, source_target_pairs={{0,64},{64,128},{128,192},{192,256},{256,320},{320,384},{384,448},... | collective-permute-start | bytes 668168 | tf_op jit(solution)/shard_map/ppermute | solution.py:240
  186.9 24.6 %collective-permute-start.22 = (bf16[145,768]{1,0:T(8,128)(2,1)S(1)}, bf16[145,768]{1,0:T(8,128)(2,1)S(1)}, u32[]{:S(2)}, u32[]{:S(2)}) collective-permute-start(bf16[145,768]{1,0:T(8,128)(2,1)S(1)} %slice.41), channel_id=1, source_target_pairs={{64,0},{128,448},{65,1},{129,449},{66,2},{130,450},{67,3},{131,451... | collective-permute-start | bytes 668168 | tf_op jit(solution)/shard_map/ppermute | solution.py:240
  (16 other events, 56.8 us)
Sparse Core Ops, SparseCore 0:
  17.7 35.6 reduce-scatter.1
  94.7 52.8 all-gather.2

commit v2 on v1

v2 whole, which is shorter than its diff:
```python
import math

import jax
import jax.numpy as jnp
import numpy as np
from jax import lax
from jax.experimental import pallas as pl
from jax.experimental.pallas import tpu as pltpu
from jax.sharding import Mesh
from jax.sharding import PartitionSpec as P

D = 768
HEADS = 12
HEAD_DIM = 64
SEQ = 257
PAD = 272
KEYS = 384
HALF = D // 2
EARLY = 128
DIRECT = 384
SWAPS = 4
SECTIONS = 8
REPLICAS = 64
AXES = ("x", "yh", "z", "yl", "c")
SECTION = ("x", "yh")


def time_rows(timestep):
    half_width = D // 2
    frequency = jnp.exp(
        -math.log(10000.0) * jnp.arange(half_width).astype(jnp.float32) / half_width
    )
    angles = timestep.astype(jnp.float32)[:, None] * frequency[None, :]
    return jnp.concatenate([jnp.cos(angles), jnp.sin(angles)], axis=1).astype(jnp.bfloat16)


def gathered(mine, other, start, count):
    def rows(ref):
        return ref[:, start : start + count, :].reshape(-1, HALF)

    return jnp.concatenate(
        [rows(mine), jnp.concatenate([rows(ref) for ref in other], axis=0)], axis=1
    )


def block_kernel(place_ref, time_ref, gain_ref, mine, *refs):
    other, refs = refs[:SWAPS], refs[SWAPS:]
    early, late, direct, around, out_ref, *refs = refs
    entering_rows, skip_rows, out_rows, block_in, qkv_rows, context = refs
    images = entering_rows.shape[0]
    section = place_ref[1]
    decoder = (section == 0) | (section >= 5)
    first_half = pl.multiple_of(place_ref[0] * HALF, 128)
    second_half = pl.multiple_of(HALF - place_ref[0] * HALF, 128)
    natural = ((first_half, 0), (second_half, HALF))
    qkv_rows[...] = jnp.zeros_like(qkv_rows)
    context[...] = jnp.zeros_like(context)

    def assemble(rows, image, head, tail):
        start, stop = SEQ * image, SEQ * image + SEQ
        split = head.shape[0]
        cut = min(max(split, start), stop)
        if start < cut:
            rows[image, : cut - start] = head[start:cut]
        if cut < stop:
            rows[image, cut - start :] = tail[cut - split : stop - split]

    for image in range(images):
        assemble(entering_rows, image, early, late)

        @pl.when(section == 1)
        def _():
            entering_rows[image, :1] = time_ref[image].astype(jnp.bfloat16)

        @pl.when(section == 5)
        def _():
            skip_rows[image] = entering_rows[image]

        @pl.when(decoder & (section != 5))
        def _():
            assemble(skip_rows, image, direct, around)

    def one_image(image):
        entering = entering_rows[image]

        @pl.when(decoder)
        def _():
            join = gathered(mine, other, 4 * 96, 192)
            mixed = jnp.dot(entering, join[:D], preferred_element_type=jnp.float32)
            mixed = mixed + jnp.dot(
                skip_rows[image], join[D:], preferred_element_type=jnp.float32
            )
            for here, start in natural:
                block_in[:, pl.ds(here, HALF)] = mixed[:, start : start + HALF].astype(
                    jnp.bfloat16
                )

        @pl.when(jnp.logical_not(decoder))
        def _():
            block_in[...] = entering

        floats = block_in[...].astype(jnp.float32)
        center = jnp.mean(floats, axis=-1, keepdims=True)
        moved = floats - center
        spread = jnp.mean(jnp.square(moved), axis=-1, keepdims=True)
        normed = (moved * lax.rsqrt(spread + 1e-05) * gain_ref[...]).astype(jnp.bfloat16)
        for part in range(3):
            columns = slice(D * part, D * part + D)
            qkv_rows[:SEQ, columns] = jnp.dot(
                normed,
                gathered(mine, other, 96 * part, 96),
                preferred_element_type=jnp.float32,
            ).astype(jnp.bfloat16)

        low_q = lax.broadcasted_iota(jnp.int32, (PAD, 128), 1) < HEAD_DIM
        low_k = lax.broadcasted_iota(jnp.int32, (KEYS, 128), 1) < HEAD_DIM
        real = lax.broadcasted_iota(jnp.int32, (PAD, 128), 1) == 0
        zero = jnp.zeros((), jnp.bfloat16)
        one = jnp.ones((), jnp.bfloat16)
        for pair in range(HEADS // 2):
            lanes = slice(128 * pair, 128 * pair + 128)
            queries = qkv_rows[:PAD, lanes]
            keys = qkv_rows[:, D + 128 * pair : D + 128 * pair + 128]
            values = qkv_rows[:, 2 * D + 128 * pair : 2 * D + 128 * pair + 128]
            sums = []
            for low in (True, False):
                here_q = low_q if low else jnp.logical_not(low_q)
                here_k = low_k if low else jnp.logical_not(low_k)
                scores = lax.dot_general(
                    jnp.where(here_q, queries, zero),
                    keys,
                    (((1,), (1,)), ((), ())),
                    preferred_element_type=jnp.float32,
                )
                main, last = scores[:, :256], jnp.where(real, scores[:, 256:], -1e30)
                row_max = jnp.maximum(
                    jnp.max(main, axis=-1, keepdims=True), jnp.max(last, axis=-1, keepdims=True)
                )
                factor = HEAD_DIM ** (-0.5) * math.log2(math.e)
                powered = jnp.concatenate(
                    [jnp.exp2((main - row_max) * factor), jnp.exp2((last - row_max) * factor)], axis=1
                ).astype(jnp.bfloat16)
                sums.append(
                    jnp.dot(powered, jnp.where(here_k, values, one), preferred_element_type=jnp.float32)
                )
            own = jnp.where(low_q, sums[0], sums[1])
            total = pltpu.roll(jnp.where(low_q, sums[1], sums[0]), HEAD_DIM, 1)
            here, start = natural[pair // 3]
            column = pl.multiple_of(here + (128 * pair - start), 128)
            context[:, pl.ds(column, 128)] = (own / total).astype(jnp.bfloat16)

        projected = jnp.dot(
            context[:SEQ], gathered(mine, other, 3 * 96, 96), preferred_element_type=jnp.float32
        )
        for here, start in natural:
            columns = pl.ds(here, HALF)
            out_rows[image, :, columns] = (
                block_in[:, columns].astype(jnp.float32) + projected[:, start : start + HALF]
            ).astype(jnp.bfloat16)

    pl.loop(0, images)(one_image)
    for image in range(images):
        out_ref[SEQ * image : SEQ * image + SEQ] = out_rows[image]


def run_block(place, times, gain_row, mine, other, early, late, direct, around):
    whole = pl.BlockSpec(memory_space=pltpu.VMEM)
    rows = early.shape[0] + late.shape[0]
    images = rows // SEQ
    return pl.pallas_call(
        block_kernel,
        out_shape=jax.ShapeDtypeStruct((rows, D), jnp.bfloat16),
        in_specs=[pl.BlockSpec(memory_space=pltpu.SMEM)] + [whole] * (7 + SWAPS),
        out_specs=whole,
        scratch_shapes=[
            pltpu.VMEM((images, SEQ, D), jnp.bfloat16),
            pltpu.VMEM((images, SEQ, D), jnp.bfloat16),
            pltpu.VMEM((images, SEQ, D), jnp.bfloat16),
            pltpu.VMEM((SEQ, D), jnp.bfloat16),
            pltpu.VMEM((KEYS, 3 * D), jnp.bfloat16),
            pltpu.VMEM((PAD, D), jnp.bfloat16),
        ],
        compiler_params=pltpu.CompilerParams(vmem_limit_bytes=28 * 2**20),
        cost_estimate=pl.CostEstimate(
            flops=images * 2 * SEQ * D * D * 7, bytes_accessed=12 * 2**20, transcendentals=0
        ),
    )(place, times, gain_row, mine, *other, early, late, direct, around)


def arrival_places(core):
    slot = np.arange(576)
    deep = slot >= 384
    row = np.where(deep, slot - 384, slot % 96)
    depth = np.where(deep, 24, 12)
    arrival = (row // depth) % 2 ^ core
    packed = np.where(deep, 48, slot // 96 * 12) + row % depth
    return ((row // (2 * depth) * 2 + arrival) * 72 + packed).astype(np.int32)


def on_device(
    stream_in, timestep, ln_gain, qkv_weight, out_weight, join_weight, ctx_saved, out_cot
):
    section = lax.axis_index(SECTION)
    core = lax.axis_index("c")
    y_low = lax.axis_index("yl")
    place = jnp.stack([core, section]).astype(jnp.int32)
    onward = [(s, (s + 1) % SECTIONS) for s in range(SECTIONS)]
    swap = [(0, 1), (1, 0)]

    term = lax.dot_general(
        ctx_saved[0], out_cot[0], (((0,), (0,)), ((), ())), preferred_element_type=jnp.float32
    )
    level = lax.psum_scatter(term, "z", scatter_dimension=0, tiled=True)

    join_rows = lax.dynamic_index_in_dim(
        join_weight, jnp.clip(section - 4, 0, 3), 0, keepdims=False
    )

    def pack(half):
        columns = HALF * half
        qkv = lax.dynamic_slice_in_dim(qkv_weight[0].reshape(12, 3, D), columns, HALF, 2)
        return jnp.concatenate(
            [
                qkv.transpose(1, 0, 2).reshape(36, HALF),
                lax.dynamic_slice_in_dim(out_weight[0], columns, HALF, 1),
                lax.dynamic_slice_in_dim(join_rows, columns, HALF, 1),
            ],
            axis=0,
        )

    own_pack, cross_pack, whole = lax.optimization_barrier(
        (pack(core), pack(1 - core), stream_in[0])
    )
    straight = lax.ppermute(own_pack, SECTION, onward)
    crossed = lax.ppermute(
        cross_pack,
        AXES,
        [
            (i, ((i // REPLICAS + 1) % SECTIONS) * REPLICAS + ((i % REPLICAS) ^ 1))
            for i in range(SECTIONS * REPLICAS)
        ],
    )
    pair = jnp.concatenate([straight, crossed], axis=0)
    places = jnp.where(core == 0, arrival_places(0), arrival_places(1))
    source = lax.broadcasted_iota(jnp.int32, (576, 576), 1)
    order = (source == places[:, None]).astype(jnp.bfloat16)
    order, pair, gain = lax.optimization_barrier((order, pair, ln_gain))
    near = lax.all_gather(pair, "yl", axis=0, tiled=True)
    near = jnp.dot(
        order, near, preferred_element_type=jnp.float32
    ).astype(jnp.bfloat16)

    early = lax.ppermute(whole[:EARLY], SECTION, onward)
    gain_row = lax.ppermute(gain, SECTION, onward)
    moved = lax.ppermute(whole[DIRECT:], SECTION, [(1, 7), (2, 6), (3, 5)])

    near, whole, gain_row, moved, early = lax.optimization_barrier(
        (near, whole, gain_row, moved, early)
    )
    mine = lax.all_gather(near, "z", axis=0, tiled=False)
    late = lax.ppermute(whole[EARLY:], SECTION, onward)
    direct = lax.ppermute(whole[:DIRECT], SECTION, [(1, 0), (2, 7), (3, 6)])
    around = lax.ppermute(moved, SECTION, [(5, 6), (6, 7), (7, 0)])
    mine, direct, around = lax.optimization_barrier((mine, direct, around))
    other = [
        lax.ppermute(part, "c", swap) for part in jnp.split(mine, SWAPS, axis=0)
    ]

    times = time_rows(timestep).astype(jnp.float32).reshape(-1, 1, D)
    stream_out = run_block(place, times, gain_row, mine, other, early, late, direct, around)

    level = level.reshape(4, 2, 12, D)
    halves = [level[:, 0].reshape(48, D), level[:, 1].reshape(48, D)]
    level = jnp.where(core == 0, *halves) + lax.ppermute(
        jnp.where(core == 0, *halves[::-1]), "c", swap
    )
    level = level.reshape(4, 12, D)
    pieces = lax.all_to_all(level, "yl", 0, 0, tiled=True)
    stream_out, pieces = lax.optimization_barrier((stream_out, pieces))
    weight_grad = jnp.sum(pieces.reshape(4, 12, D), axis=0)
    return (stream_out[None], weight_grad[None])


def solution(mesh):
    fine = Mesh(mesh.devices.reshape(4, 2, 8, 4, 2), AXES)
    section, dp = ("x", "yh"), ("z", "yl", "c")
    return jax.shard_map(
        on_device,
        mesh=fine,
        in_specs=(
            P(section, dp, None),
            P(dp),
            P(section, None),
            P(section, dp, None),
            P(section, dp, None),
            P(None, dp, None),
            P(section, dp, None),
            P(section, dp, None),
        ),
        out_specs=(P(section, dp, None), P(section, dp, None)),
        check_vma=False,
    )
```

time: 233 us -> 173 us (0.74)
  the two profiles are of different devices: /device:TPU:373 before, /device:TPU:196 now
where the time goes in v2:
time: 173 us; the launch traced here: 172 us
  starting transfers between devices  50 us (29%)
  waiting for transfers between devices  43.6 us (25%)
  local copies, waits for them, and re-layouts  21.9 us (13%)
  blocking collectives  16.7 us (10%)
  Pallas kernels  16.1 us (9%)
  between operations  14.5 us (8%)
  matrix products  5.47 us (3%)
  other arithmetic  3.89 us (2%)
    all_gather x1, waiting for transfers between devices, on_device(): mine = lax.all_gather(near, 'z', axis=0, tiled=False)  32.6 us
    all_gather x1, blocking collectives, on_device(): near = lax.all_gather(pair, 'yl', axis=0, tiled=True)  16.7 us
    pallas_call x1, Pallas kernels, run_block(): pl.pallas_call(block_kernel, out_shape=jax.ShapeDtypeStruct((rows, D), jn...  16.1 us
    ppermute x1, starting transfers between devices, on_device(): late = lax.ppermute(whole[EARLY:], SECTION, onward)  12.8 us
    ppermute x1, waiting for transfers between devices, on_device(): late = lax.ppermute(whole[EARLY:], SECTION, onward)  9.16 us
    ppermute x4, starting transfers between devices, on_device(): lax.ppermute(part, 'c', swap)  8.79 us
    ppermute x1, starting transfers between devices, on_device(): early = lax.ppermute(whole[:EARLY], SECTION, onward)  7.61 us
    ppermute x1, starting transfers between devices, on_device(): straight = lax.ppermute(own_pack, SECTION, onward)  7.54 us
  transfers between devices with their start and end apart: 16, of which 3 were waited for; matrix products, arithmetic and copies ran while one was open for 12% of the time, Pallas kernels for 9%

profile of v2, /device:TPU:196, one launch (start us, length us, event | category | flops | bytes accessed | tf_op | source)
XLA Modules:
  0.0 172.1 jit_solution(15052877143889560104)
XLA Ops:
  7.2 1.2 copy-done
  8.4 4.1 %fusion.1 = f32[768,768]{1,0:T(8,128)} fusion(bf16[1,771,768]{2,1,0:T(8,128)(2,1)S(1)} %copy-done, bf16[1,771,768]{2,1,0:T(8,128)(2,1)} %param.16), kind=kOutput, calls=%fused_computation.3 | convolution fusion | flops 909508608 | bytes 4727808 | tf_op jit(solution)/shard_map/dot_general | solution.py:210
  14.7 1.5 collective-permute-start.3
  16.2 7.5 %collective-permute-start = (bf16[72,384]{1,0:T(8,128)(2,1)S(1)}, bf16[72,384]{1,0:T(8,128)(2,1)S(1)}, u32[]{:S(2)}, u32[]{:S(2)}) collective-permute-start(bf16[72,384]{1,0:T(8,128)(2,1)S(1)} %get-tuple-element.18), channel_id=1, source_target_pairs={{0,64},{64,128},{128,192},{192,256},{256,320},{320,384},{384,448},... | collective-permute-start | bytes 165896 | tf_op jit(solution)/shard_map/ppermute | solution.py:234
  23.7 1.9 %collective-permute-start.1 = (bf16[72,384]{1,0:T(8,128)(2,1)S(1)}, bf16[72,384]{1,0:T(8,128)(2,1)S(1)}, u32[]{:S(2)}, u32[]{:S(2)}) collective-permute-start(bf16[72,384]{1,0:T(8,128)(2,1)S(1)} %get-tuple-element.19), channel_id=1, source_target_pairs={{0,65},{1,64},{2,67},{3,66},{4,69},{5,68},{6,71},{7,70},{8,73},{9,... | collective-permute-start | bytes 165896 | tf_op jit(solution)/shard_map/ppermute | solution.py:235
  25.7 7.6 %collective-permute-start.4 = (bf16[128,768]{1,0:T(8,128)(2,1)S(1)}, bf16[128,768]{1,0:T(8,128)(2,1)S(1)}, u32[]{:S(2)}, u32[]{:S(2)}) collective-permute-start(bf16[128,768]{1,0:T(8,128)(2,1)S(1)} %slice.19), channel_id=1, source_target_pairs={{0,64},{64,128},{128,192},{192,256},{256,320},{320,384},{384,448},... | collective-permute-start | bytes 589832 | tf_op jit(solution)/shard_map/ppermute | solution.py:253
  33.5 1.8 %collective-permute-done.1 = bf16[72,384]{1,0:T(8,128)(2,1)S(1)} collective-permute-done((bf16[72,384]{1,0:T(8,128)(2,1)S(1)}, bf16[72,384]{1,0:T(8,128)(2,1)S(1)}, u32[]{:S(2)}, u32[]{:S(2)}) %collective-permute-start.1) | collective-permute-done | bytes 55328 | tf_op jit(solution)/shard_map/ppermute | solution.py:235
  35.3 1.9 %collective-permute-start.2 = (f32[1,768]{1,0:T(1,128)S(1)}, f32[1,768]{1,0:T(1,128)S(1)}, u32[]{:S(2)}, u32[]{:S(2)}) collective-permute-start(f32[1,768]{1,0:T(1,128)S(1)} %copy-done.14), channel_id=1, source_target_pairs={{0,64},{64,128},{128,192},{192,256},{256,320},{320,384},{384,448},... | collective-permute-start | bytes 9224 | tf_op jit(solution)/shard_map/ppermute | solution.py:254
  37.2 16.7 %all_gather.9 = bf16[576,384]{1,0:T(8,128)(2,1)S(1)} all-gather(bf16[144,384]{1,0:T(8,128)(2,1)S(1)} %pad_maximum_fusion), channel_id=1, replica_groups=mesh['x'=4,'yh'=2,'z'=8,'yl'=4,'c'=2] {'yl'}, dimensions={0}, use_global_device_ids=true | all-gather | bytes 552960 | tf_op jit(solution)/shard_map/all_gather | solution.py:248
  53.9 1.3 convolution_convert_fusion
  56.0 1.9 %slice.20 = bf16[384,768]{1,0:T(8,128)(2,1)} slice(bf16[771,768]{1,0:T(8,128)(2,1)} %bitcast.33), slice={[0:384], [0:768]} | slice | bytes 1179648 | tf_op jit(solution)/shard_map/slice | solution.py:262
  58.6 2.2 %slice.21 = bf16[643,768]{1,0:T(8,128)(2,1)} slice(bf16[771,768]{1,0:T(8,128)(2,1)} %bitcast.34), slice={[128:771], [0:768]} | slice | bytes 1975296 | tf_op jit(solution)/shard_map/slice | solution.py:261
  60.8 12.8 %collective-permute-start.11 = (bf16[643,768]{1,0:T(8,128)(2,1)}, bf16[643,768]{1,0:T(8,128)(2,1)S(1)}, u32[]{:S(2)}, u32[]{:S(2)}) collective-permute-start(bf16[643,768]{1,0:T(8,128)(2,1)} %slice.21), channel_id=1, source_target_pairs={{0,64},{64,128},{128,192},{192,256},{256,320},{320,384},{384,448},... | collective-permute-start | bytes 2962952 | tf_op jit(solution)/shard_map/ppermute | solution.py:261
  73.7 1.7 %reshape.117 = f32[4,2,12,768]{3,2,1,0:T(8,128)} reshape(f32[96,768]{1,0:T(8,128)} %reduce-scatter.2.cloned.1.call-done) | data formatting | bytes 589824 | tf_op jit(solution)/shard_map/reshape | solution.py:272
  75.4 1.8 %slice_select_fusion = (f32[4,1,12,768]{3,2,1,0:T(8,128)}, f32[4,1,12,768]{3,2,1,0:T(8,128)}) fusion(f32[4,2,12,768]{3,2,1,0:T(8,128)} %reshape.117, pred[]{:T(512)S(6)} %eq.6), kind=kLoop, calls=%fused_computation.6 | loop fusion | flops 73728 | bytes 589825 | tf_op jit(solution)/shard_map/jit(_where)/select_n | solution.py:275
  77.2 1.6 select_n.52
  78.8 1.9 %collective-permute-start.12 = (f32[48,768]{1,0:T(8,128)}, f32[48,768]{1,0:T(8,128)S(1)}, u32[]{:S(2)}, u32[]{:S(2)}) collective-permute-start(f32[48,768]{1,0:T(8,128)} %select_n.52), channel_id=1, source_target_pairs={{0,1},{1,0},{2,3},{3,2},{4,5},{5,4},{6,7},{7,6},{8,9},{9,8},{10,11... | collective-permute-start | bytes 442376 | tf_op jit(solution)/shard_map/ppermute | solution.py:274
  80.8 32.6 %all-gather.3.cloned.1.call-done = bf16[4608,384]{1,0:T(8,128)(2,1)} async-done(((bf16[576,384]{1,0:T(8,128)(2,1)}), bf16[4608,384]{1,0:T(8,128)(2,1)}) %all-gather.3.cloned.1.call-update) | async-done | bytes 3538960 | tf_op jit(solution)/shard_map/all_gather | solution.py:260
  113.4 3.9 %fusion.8 = (bf16[2,576,384]{2,1,0:T(8,128)(2,1)}, bf16[2,576,384]{2,1,0:T(8,128)(2,1)}, bf16[2,576,384]{2,1,0:T(8,128)(2,1)}, bf16[2,576,384]{2,1,0:T(8,128)(2,1)}) fusion(bf16[8,576,384]{2,1,0:T(8,128)(2,1)} %bitcast.31), kind=kLoop, calls=%fused_computation.29 | loop fusion | bytes 7077888 | tf_op jit(solution)/shard_map/split | solution.py:266
  117.3 2.1 %collective-permute-start.10 = (bf16[2,576,384]{2,1,0:T(8,128)(2,1)}, bf16[2,576,384]{2,1,0:T(8,128)(2,1)S(1)}, u32[]{:S(2)}, u32[]{:S(2)}) collective-permute-start(bf16[2,576,384]{2,1,0:T(8,128)(2,1)} %get-tuple-element.34), channel_id=1, source_target_pairs={{0,1},{1,0},{2,3},{3,2},{4,5},{5,4},{6,7},{7,6},{8,9},{9,8},{10,11... | collective-permute-start | bytes 2654216 | tf_op jit(solution)/shard_map/ppermute | solution.py:266
  119.4 2.4 %collective-permute-start.7 = (bf16[2,576,384]{2,1,0:T(8,128)(2,1)}, bf16[2,576,384]{2,1,0:T(8,128)(2,1)}, u32[]{:S(2)}, u32[]{:S(2)}) collective-permute-start(bf16[2,576,384]{2,1,0:T(8,128)(2,1)} %get-tuple-element.37), channel_id=1, source_target_pairs={{0,1},{1,0},{2,3},{3,2},{4,5},{5,4},{6,7},{7,6},{8,9},{9,8},{10,11... | collective-permute-start | bytes 2654216 | tf_op jit(solution)/shard_map/ppermute | solution.py:266
  121.8 1.9 %collective-permute-start.8 = (bf16[2,576,384]{2,1,0:T(8,128)(2,1)}, bf16[2,576,384]{2,1,0:T(8,128)(2,1)}, u32[]{:S(2)}, u32[]{:S(2)}) collective-permute-start(bf16[2,576,384]{2,1,0:T(8,128)(2,1)} %get-tuple-element.36), channel_id=1, source_target_pairs={{0,1},{1,0},{2,3},{3,2},{4,5},{5,4},{6,7},{7,6},{8,9},{9,8},{10,11... | collective-permute-start | bytes 2654216 | tf_op jit(solution)/shard_map/ppermute | solution.py:266
  123.7 2.4 %collective-permute-start.9 = (bf16[2,576,384]{2,1,0:T(8,128)(2,1)}, bf16[2,576,384]{2,1,0:T(8,128)(2,1)}, u32[]{:S(2)}, u32[]{:S(2)}) collective-permute-start(bf16[2,576,384]{2,1,0:T(8,128)(2,1)} %get-tuple-element.35), channel_id=1, source_target_pairs={{0,1},{1,0},{2,3},{3,2},{4,5},{5,4},{6,7},{7,6},{8,9},{9,8},{10,11... | collective-permute-start | bytes 2654216 | tf_op jit(solution)/shard_map/ppermute | solution.py:266
  126.4 0.9 select_n.50
  127.4 1.6 add.30
  129.0 1.6 reshape.118
  130.6 4.6 %all-to-all-start = ((f32[4,12,768]{2,1,0:T(8,128)}), f32[4,12,768]{2,1,0:T(8,128)S(1)}, u32[]{:S(2)}, u32[]{:S(2)}) async-start(f32[4,12,768]{2,1,0:T(8,128)} %reshape.118), calls=%async_computation.1 | async-start | bytes 393216 | tf_op jit(solution)/shard_map/all_to_all | solution.py:278
  135.2 9.2 %collective-permute-done.11.refs_5_ = bf16[643,768]{1,0:T(8,128)(2,1)S(1)} collective-permute-done((bf16[643,768]{1,0:T(8,128)(2,1)}, bf16[643,768]{1,0:T(8,128)(2,1)S(1)}, u32[]{:S(2)}, u32[]{:S(2)}) %collective-permute-start.11) | collective-permute-done | bytes 987680 | tf_op jit(solution)/shard_map/ppermute | solution.py:261
  144.4 2.0 %copy-done.1 = bf16[4608,384]{1,0:T(8,128)(2,1)S(1)} copy-done((bf16[4608,384]{1,0:T(8,128)(2,1)S(1)}, bf16[4608,384]{1,0:T(8,128)(2,1)}, u32[]{:S(2)}) %copy-start.1) | copy-done | bytes 3538968
  146.4 1.1 copy-done.3
  147.5 1.1 copy-done.5
  148.5 16.1 %shard_map.113 = bf16[771,768]{1,0:T(8,128)(2,1)} custom-call(s32[2]{0:T(128)S(1)} %pad_add_fusion.place_ref, f32[3,1,768]{2,1,0:T(1,128)S(1)} %maximum_convert_fusion.time_ref, f32[1,768]{1,0:T(1,128)S(1)} %collective-permute-done.2.gain_ref, bf16[8,576,384]{2,1,0:T(8,128)(2,1)S(1)} %bitcast.32, bf16[2,576,384]{2,1,0:T(8,128)(2,1)} %collective-permute-done.7.refs_0_, ...), custom_call_target="tpu_custom_call" | custom-call | flops 6366560256 | bytes 12582912 | tf_op jit(solution)/shard_map/pallas_call | solution.py:170
  (70 shorter events, 4.6 us)
Async XLA Ops:
  7.2 1.3 copy-start
  7.2 66.5 %reduce-scatter.2.cloned.1.call-start = ((), (), s32[]{:S(2)}) async-start(), calls=%async_computation.2 | async-start | bytes 2654208 | tf_op jit(solution)/shard_map/reduce_scatter | solution.py:213
  12.6 0.9 copy-start.10
  12.6 1.1 copy-start.11
  12.6 2.0 %copy-start.8 = (bf16[1,771,768]{2,1,0:T(8,128)(2,1)S(1)}, bf16[1,771,768]{2,1,0:T(8,128)(2,1)}, u32[]{:S(2)}) copy-start(bf16[1,771,768]{2,1,0:T(8,128)(2,1)} %param.10) | copy-start | bytes 3552772
  12.6 100.8 %all-gather.3.cloned.1.call-start = ((), (), s32[]{:S(2)}) async-start(), calls=%async_computation.3 | async-start | bytes 3981312 | tf_op jit(solution)/shard_map/all_gather | solution.py:260
  13.5 19.8 %copy-start.12 = (s32[576]{0:T(1024)S(1)}, s32[576]{0:T(1024)}, u32[]{:S(2)}) copy-start(s32[576]{0:T(1024)} %constant.79.clone) | copy-start | bytes 6916
  13.5 19.8 %copy-start.13 = (s32[576]{0:T(1024)S(1)}, s32[576]{0:T(1024)}, u32[]{:S(2)}) copy-start(s32[576]{0:T(1024)} %constant.80.clone) | copy-start | bytes 6916
  14.6 20.7 %copy-start.14 = (f32[1,768]{1,0:T(1,128)S(1)}, f32[1,768]{1,0:T(1,128)}, u32[]{:S(2)}) copy-start(f32[1,768]{1,0:T(1,128)} %param.12) | copy-start | bytes 9220
  14.7 40.6 %collective-permute-start.3 = (bf16[387,768]{1,0:T(8,128)(2,1)S(1)}, bf16[387,768]{1,0:T(8,128)(2,1)}, u32[]{:S(2)}, u32[]{:S(2)}) collective-permute-start(bf16[387,768]{1,0:T(8,128)(2,1)S(1)} %slice.18), channel_id=1, source_target_pairs={{64,448},{128,384},{192,320},{65,449},{129,385},{193,321},{66,450}... | collective-permute-start | bytes 1783304 | tf_op jit(solution)/shard_map/ppermute | solution.py:255
  16.2 17.4 %collective-permute-start = (bf16[72,384]{1,0:T(8,128)(2,1)S(1)}, bf16[72,384]{1,0:T(8,128)(2,1)S(1)}, u32[]{:S(2)}, u32[]{:S(2)}) collective-permute-start(bf16[72,384]{1,0:T(8,128)(2,1)S(1)} %get-tuple-element.18), channel_id=1, source_target_pairs={{0,64},{64,128},{128,192},{192,256},{256,320},{320,384},{384,448},... | collective-permute-start | bytes 165896 | tf_op jit(solution)/shard_map/ppermute | solution.py:234
  23.7 11.6 %collective-permute-start.1 = (bf16[72,384]{1,0:T(8,128)(2,1)S(1)}, bf16[72,384]{1,0:T(8,128)(2,1)S(1)}, u32[]{:S(2)}, u32[]{:S(2)}) collective-permute-start(bf16[72,384]{1,0:T(8,128)(2,1)S(1)} %get-tuple-element.19), channel_id=1, source_target_pairs={{0,65},{1,64},{2,67},{3,66},{4,69},{5,68},{6,71},{7,70},{8,73},{9,... | collective-permute-start | bytes 165896 | tf_op jit(solution)/shard_map/ppermute | solution.py:235
  25.7 29.6 %collective-permute-start.4 = (bf16[128,768]{1,0:T(8,128)(2,1)S(1)}, bf16[128,768]{1,0:T(8,128)(2,1)S(1)}, u32[]{:S(2)}, u32[]{:S(2)}) collective-permute-start(bf16[128,768]{1,0:T(8,128)(2,1)S(1)} %slice.19), channel_id=1, source_target_pairs={{0,64},{64,128},{128,192},{192,256},{256,320},{320,384},{384,448},... | collective-permute-start | bytes 589832 | tf_op jit(solution)/shard_map/ppermute | solution.py:253
  35.3 19.9 %collective-permute-start.2 = (f32[1,768]{1,0:T(1,128)S(1)}, f32[1,768]{1,0:T(1,128)S(1)}, u32[]{:S(2)}, u32[]{:S(2)}) collective-permute-start(f32[1,768]{1,0:T(1,128)S(1)} %copy-done.14), channel_id=1, source_target_pairs={{0,64},{64,128},{128,192},{192,256},{256,320},{320,384},{384,448},... | collective-permute-start | bytes 9224 | tf_op jit(solution)/shard_map/ppermute | solution.py:254
  55.2 3.4 %copy-start.6 = (bf16[128,768]{1,0:T(8,128)(2,1)}, bf16[128,768]{1,0:T(8,128)(2,1)S(1)}, u32[]{:S(2)}) copy-start(bf16[128,768]{1,0:T(8,128)(2,1)S(1)} %collective-permute-done.4.refs_4_) | copy-start | bytes 589828
  55.3 25.5 %collective-permute-start.6 = (bf16[387,768]{1,0:T(8,128)(2,1)}, bf16[387,768]{1,0:T(8,128)(2,1)S(1)}, u32[]{:S(2)}, u32[]{:S(2)}) collective-permute-start(bf16[387,768]{1,0:T(8,128)(2,1)} %collective-permute-done.3), channel_id=1, source_target_pairs={{320,384},{384,448},{448,0},{321,385},{385,449},{449,1},{322,386},... | collective-permute-start | bytes 1783304 | tf_op jit(solution)/shard_map/ppermute | solution.py:263
  57.9 22.9 %collective-permute-start.5 = (bf16[384,768]{1,0:T(8,128)(2,1)}, bf16[384,768]{1,0:T(8,128)(2,1)S(1)}, u32[]{:S(2)}, u32[]{:S(2)}) collective-permute-start(bf16[384,768]{1,0:T(8,128)(2,1)} %slice.20), channel_id=1, source_target_pairs={{64,0},{128,448},{192,384},{65,1},{129,449},{193,385},{66,2},{130,... | collective-permute-start | bytes 1769480 | tf_op jit(solution)/shard_map/ppermute | solution.py:262
  60.8 83.5 %collective-permute-start.11 = (bf16[643,768]{1,0:T(8,128)(2,1)}, bf16[643,768]{1,0:T(8,128)(2,1)S(1)}, u32[]{:S(2)}, u32[]{:S(2)}) collective-permute-start(bf16[643,768]{1,0:T(8,128)(2,1)} %slice.21), channel_id=1, source_target_pairs={{0,64},{64,128},{128,192},{192,256},{256,320},{320,384},{384,448},... | collective-permute-start | bytes 2962952 | tf_op jit(solution)/shard_map/ppermute | solution.py:261
  78.8 44.9 %collective-permute-start.12 = (f32[48,768]{1,0:T(8,128)}, f32[48,768]{1,0:T(8,128)S(1)}, u32[]{:S(2)}, u32[]{:S(2)}) collective-permute-start(f32[48,768]{1,0:T(8,128)} %select_n.52), channel_id=1, source_target_pairs={{0,1},{1,0},{2,3},{3,2},{4,5},{5,4},{6,7},{7,6},{8,9},{9,8},{10,11... | collective-permute-start | bytes 442376 | tf_op jit(solution)/shard_map/ppermute | solution.py:274
  80.8 36.5 %copy-start.4 = (bf16[384,768]{1,0:T(8,128)(2,1)}, bf16[384,768]{1,0:T(8,128)(2,1)S(1)}, u32[]{:S(2)}) copy-start(bf16[384,768]{1,0:T(8,128)(2,1)S(1)} %collective-permute-done.5.refs_6_) | copy-start | bytes 1769476
  80.8 36.5 %copy-start.2 = (bf16[387,768]{1,0:T(8,128)(2,1)}, bf16[387,768]{1,0:T(8,128)(2,1)S(1)}, u32[]{:S(2)}) copy-start(bf16[387,768]{1,0:T(8,128)(2,1)S(1)} %collective-permute-done.6.refs_7_) | copy-start | bytes 1783300
  113.4 12.8 %copy-start.15 = (s32[3]{0:T(128)S(1)}, s32[3]{0:T(128)}, u32[]{:S(2)}) copy-start(s32[3]{0:T(128)} %param.11) | copy-start | bytes 40
  117.3 27.1 %copy-start.7 = (bf16[128,768]{1,0:T(8,128)(2,1)S(1)}, bf16[128,768]{1,0:T(8,128)(2,1)}, u32[]{:S(2)}) copy-start(bf16[128,768]{1,0:T(8,128)(2,1)} %copy-done.6) | copy-start | bytes 589828
  117.3 27.1 %collective-permute-start.10 = (bf16[2,576,384]{2,1,0:T(8,128)(2,1)}, bf16[2,576,384]{2,1,0:T(8,128)(2,1)S(1)}, u32[]{:S(2)}, u32[]{:S(2)}) collective-permute-start(bf16[2,576,384]{2,1,0:T(8,128)(2,1)} %get-tuple-element.34), channel_id=1, source_target_pairs={{0,1},{1,0},{2,3},{3,2},{4,5},{5,4},{6,7},{7,6},{8,9},{9,8},{10,11... | collective-permute-start | bytes 2654216 | tf_op jit(solution)/shard_map/ppermute | solution.py:266
  119.4 25.0 %collective-permute-start.7 = (bf16[2,576,384]{2,1,0:T(8,128)(2,1)}, bf16[2,576,384]{2,1,0:T(8,128)(2,1)}, u32[]{:S(2)}, u32[]{:S(2)}) collective-permute-start(bf16[2,576,384]{2,1,0:T(8,128)(2,1)} %get-tuple-element.37), channel_id=1, source_target_pairs={{0,1},{1,0},{2,3},{3,2},{4,5},{5,4},{6,7},{7,6},{8,9},{9,8},{10,11... | collective-permute-start | bytes 2654216 | tf_op jit(solution)/shard_map/ppermute | solution.py:266
  121.8 22.6 %collective-permute-start.8 = (bf16[2,576,384]{2,1,0:T(8,128)(2,1)}, bf16[2,576,384]{2,1,0:T(8,128)(2,1)}, u32[]{:S(2)}, u32[]{:S(2)}) collective-permute-start(bf16[2,576,384]{2,1,0:T(8,128)(2,1)} %get-tuple-element.36), channel_id=1, source_target_pairs={{0,1},{1,0},{2,3},{3,2},{4,5},{5,4},{6,7},{7,6},{8,9},{9,8},{10,11... | collective-permute-start | bytes 2654216 | tf_op jit(solution)/shard_map/ppermute | solution.py:266
  123.7 2.7 %copy-start.9 = (f32[48,768]{1,0:T(8,128)}, f32[48,768]{1,0:T(8,128)S(1)}, u32[]{:S(2)}) copy-start(f32[48,768]{1,0:T(8,128)S(1)} %collective-permute-done.12) | copy-start | bytes 442372
  123.7 20.6 %collective-permute-start.9 = (bf16[2,576,384]{2,1,0:T(8,128)(2,1)}, bf16[2,576,384]{2,1,0:T(8,128)(2,1)}, u32[]{:S(2)}, u32[]{:S(2)}) collective-permute-start(bf16[2,576,384]{2,1,0:T(8,128)(2,1)} %get-tuple-element.35), channel_id=1, source_target_pairs={{0,1},{1,0},{2,3},{3,2},{4,5},{5,4},{6,7},{7,6},{8,9},{9,8},{10,11... | collective-permute-start | bytes 2654216 | tf_op jit(solution)/shard_map/ppermute | solution.py:266
  130.6 34.0 %all-to-all-start = ((f32[4,12,768]{2,1,0:T(8,128)}), f32[4,12,768]{2,1,0:T(8,128)S(1)}, u32[]{:S(2)}, u32[]{:S(2)}) async-start(f32[4,12,768]{2,1,0:T(8,128)} %reshape.118), calls=%async_computation.1 | async-start | bytes 393216 | tf_op jit(solution)/shard_map/all_to_all | solution.py:278
  144.4 2.0 %copy-start.1 = (bf16[4608,384]{1,0:T(8,128)(2,1)S(1)}, bf16[4608,384]{1,0:T(8,128)(2,1)}, u32[]{:S(2)}) copy-start(bf16[4608,384]{1,0:T(8,128)(2,1)} %all-gather.3.cloned.1.call-done) | copy-start | bytes 10616836
  146.4 1.1 copy-start.3
  147.5 1.1 copy-start.5
Sparse Core Ops, SparseCore 0:
  12.7 47.8 reduce-scatter.1
  62.7 50.6 all-gather.2

commit v3 on v2

v3 whole, which is shorter than its diff:
```python
import math

import jax
import jax.numpy as jnp
import numpy as np
from jax import lax
from jax.experimental import pallas as pl
from jax.experimental.pallas import tpu as pltpu
from jax.sharding import Mesh
from jax.sharding import PartitionSpec as P

D = 768
HEADS = 12
HEAD_DIM = 64
SEQ = 257
PAD = 272
KEYS = 384
HALF = D // 2
EARLY = 160
DIRECT = 384
SWAPS = 4
SECTIONS = 8
REPLICAS = 64
AXES = ("x", "yh", "z", "yl", "c")
SECTION = ("x", "yh")


def time_rows(timestep):
    half_width = D // 2
    frequency = jnp.exp(
        -math.log(10000.0) * jnp.arange(half_width).astype(jnp.float32) / half_width
    )
    angles = timestep.astype(jnp.float32)[:, None] * frequency[None, :]
    return jnp.concatenate([jnp.cos(angles), jnp.sin(angles)], axis=1).astype(jnp.bfloat16)


GROUPS = ((384, 192), (0, 288), (288, 96))


def weight_copies(mine, other, held, sems):
    copies = []
    for group, (start, count) in enumerate(GROUPS):
        rows = pl.ds(start, count)
        pairs = [(mine.at[:, rows], held.at[0, :, rows])]
        for i, ref in enumerate(other):
            deep = ref.shape[0]
            pairs.append((ref.at[:, rows], held.at[1, pl.ds(deep * i, deep), rows]))
        copies.append(
            [
                pltpu.make_async_copy(source, target, sems.at[group * len(pairs) + i])
                for i, (source, target) in enumerate(pairs)
            ]
        )
    return copies


def gathered(held, start, count):
    return jnp.concatenate(
        [held[half, :, start : start + count, :].reshape(-1, HALF) for half in range(2)], axis=1
    )


def block_kernel(place_ref, time_ref, gain_ref, mine, *refs):
    other, refs = refs[:SWAPS], refs[SWAPS:]
    early, late, direct, around, out_ref, *refs = refs
    held, entering, skip, block_in, normed, qkv_rows, image_context, context, sems = refs
    join_copies, qkv_copies, out_copies = weight_copies(mine, other, held, sems)
    for copy in join_copies + qkv_copies + out_copies:
        copy.start()
    count = out_ref.shape[0]
    images = count // SEQ
    section = place_ref[1]
    decoder = (section == 0) | (section >= 5)
    first_half = pl.multiple_of(place_ref[0] * HALF, 128)
    second_half = pl.multiple_of(HALF - place_ref[0] * HALF, 128)
    natural = ((first_half, 0), (second_half, HALF))
    for image in range(images):
        qkv_rows[image, 256:] = jnp.zeros((KEYS - 256, 3 * D), jnp.bfloat16)

    for copy in join_copies:
        copy.wait()

    @pl.when(decoder)
    def _():
        entering[:EARLY] = early[...]
        entering[EARLY:] = late[...]

        @pl.when(section == 5)
        def _():
            skip[...] = entering[...]

        @pl.when(section != 5)
        def _():
            skip[:DIRECT] = direct[...]
            skip[DIRECT:] = around[...]

        join = gathered(held, 4 * 96, 192)
        mixed = jnp.dot(entering[...], join[:D], preferred_element_type=jnp.float32)
        mixed = mixed + jnp.dot(skip[...], join[D:], preferred_element_type=jnp.float32)
        for here, start in natural:
            block_in[:count, pl.ds(here, HALF)] = mixed[:, start : start + HALF].astype(
                jnp.bfloat16
            )

    @pl.when(jnp.logical_not(decoder))
    def _():
        block_in[:EARLY] = early[...]
        block_in[EARLY:count] = late[...]

        @pl.when(section == 1)
        def _():
            for image in range(images):
                block_in[SEQ * image : SEQ * image + 1] = time_ref[image].astype(jnp.bfloat16)

    @pl.loop(0, block_in.shape[0] // 112)
    def _(part):
        rows = pl.ds(pl.multiple_of(part * 112, 16), 112)
        floats = block_in[rows].astype(jnp.float32)
        center = jnp.mean(floats, axis=-1, keepdims=True)
        moved = floats - center
        spread = jnp.mean(jnp.square(moved), axis=-1, keepdims=True)
        normed[rows] = (moved * lax.rsqrt(spread + 1e-05) * gain_ref[...]).astype(jnp.bfloat16)

    for copy in qkv_copies:
        copy.wait()
    for part in range(3):
        columns = slice(D * part, D * part + D)
        product = jnp.dot(
            normed[:count],
            gathered(held, 96 * part, 96),
            preferred_element_type=jnp.float32,
        ).astype(jnp.bfloat16)
        for image in range(images):
            qkv_rows[image, :SEQ, columns] = product[SEQ * image : SEQ * image + SEQ]

    @pl.loop(0, images)
    def _(image):
        low_q = lax.broadcasted_iota(jnp.int32, (PAD, 128), 1) < HEAD_DIM
        low_k = lax.broadcasted_iota(jnp.int32, (KEYS, 128), 1) < HEAD_DIM
        real = lax.broadcasted_iota(jnp.int32, (PAD, 128), 1) == 0
        zero = jnp.zeros((), jnp.bfloat16)
        one = jnp.ones((), jnp.bfloat16)
        for pair in range(HEADS // 2):
            lanes = 128 * pair
            queries = qkv_rows[image, :PAD, lanes : lanes + 128]
            keys = qkv_rows[image, :, D + lanes : D + lanes + 128]
            values = qkv_rows[image, :, 2 * D + lanes : 2 * D + lanes + 128]
            sums = []
            for low in (True, False):
                here_q = low_q if low else jnp.logical_not(low_q)
                here_k = low_k if low else jnp.logical_not(low_k)
                scores = lax.dot_general(
                    jnp.where(here_q, queries, zero),
                    keys,
                    (((1,), (1,)), ((), ())),
                    preferred_element_type=jnp.float32,
                )
                main, last = scores[:, :256], jnp.where(real, scores[:, 256:], -1e30)
                widest = jnp.maximum(jnp.maximum(main[:, :128], main[:, 128:]), last)
                row_max = jnp.max(widest, axis=-1, keepdims=True)
                factor = HEAD_DIM ** (-0.5) * math.log2(math.e)
                powered = jnp.concatenate(
                    [jnp.exp2((main - row_max) * factor), jnp.exp2((last - row_max) * factor)], axis=1
                ).astype(jnp.bfloat16)
                sums.append(
                    jnp.dot(powered, jnp.where(here_k, values, one), preferred_element_type=jnp.float32)
                )
            own = jnp.where(low_q, sums[0], sums[1])
            total = pltpu.roll(jnp.where(low_q, sums[1], sums[0]), HEAD_DIM, 1)
            here, start = natural[pair // 3]
            column = pl.multiple_of(here + (lanes - start), 128)
            image_context[image, :, pl.ds(column, 128)] = (own / total).astype(jnp.bfloat16)

    for image in range(images):
        context[SEQ * image : SEQ * image + SEQ] = image_context[image, :SEQ]
    for copy in out_copies:
        copy.wait()
    projected = jnp.dot(
        context[...], gathered(held, 3 * 96, 96), preferred_element_type=jnp.float32
    )
    for here, start in natural:
        columns = pl.ds(here, HALF)
        out_ref[:, columns] = (
            block_in[:count, columns].astype(jnp.float32) + projected[:, start : start + HALF]
        ).astype(jnp.bfloat16)


def run_block(place, times, gain_row, mine, other, early, late, direct, around):
    whole = pl.BlockSpec(memory_space=pltpu.VMEM)
    rows = early.shape[0] + late.shape[0]
    images = rows // SEQ
    return pl.pallas_call(
        block_kernel,
        out_shape=jax.ShapeDtypeStruct((rows, D), jnp.bfloat16),
        in_specs=[pl.BlockSpec(memory_space=pltpu.SMEM)]
        + [whole] * 2
        + [pl.BlockSpec(memory_space=pl.ANY)] * (1 + SWAPS)
        + [whole] * 4,
        out_specs=whole,
        scratch_shapes=[
            pltpu.VMEM((2, *mine.shape), jnp.bfloat16),
            pltpu.VMEM((rows, D), jnp.bfloat16),
            pltpu.VMEM((rows, D), jnp.bfloat16),
            pltpu.VMEM((pl.cdiv(rows, 112) * 112, D), jnp.bfloat16),
            pltpu.VMEM((pl.cdiv(rows, 112) * 112, D), jnp.bfloat16),
            pltpu.VMEM((images, KEYS, 3 * D), jnp.bfloat16),
            pltpu.VMEM((images, PAD, D), jnp.bfloat16),
            pltpu.VMEM((rows, D), jnp.bfloat16),
            pltpu.SemaphoreType.DMA((len(GROUPS) * (1 + SWAPS),)),
        ],
        compiler_params=pltpu.CompilerParams(vmem_limit_bytes=57 * 2**20),
        cost_estimate=pl.CostEstimate(
            flops=images * 2 * SEQ * D * D * 7, bytes_accessed=12 * 2**20, transcendentals=0
        ),
    )(place, times, gain_row, mine, *other, early, late, direct, around)


def arrival_places(core):
    slot = np.arange(576)
    deep = slot >= 384
    row = np.where(deep, slot - 384, slot % 96)
    depth = np.where(deep, 24, 12)
    arrival = (row // depth) % 2 ^ core
    packed = np.where(deep, 48, slot // 96 * 12) + row % depth
    return ((row // (2 * depth) * 2 + arrival) * 72 + packed).astype(np.int32)


def on_device(
    stream_in, timestep, ln_gain, qkv_weight, out_weight, join_weight, ctx_saved, out_cot
):
    section = lax.axis_index(SECTION)
    core = lax.axis_index("c")
    y_low = lax.axis_index("yl")
    place = jnp.stack([core, section]).astype(jnp.int32)
    onward = [(s, (s + 1) % SECTIONS) for s in range(SECTIONS)]
    swap = [(0, 1), (1, 0)]

    term = lax.dot_general(
        ctx_saved[0], out_cot[0], (((0,), (0,)), ((), ())), preferred_element_type=jnp.float32
    )
    level = lax.psum_scatter(term, "z", scatter_dimension=0, tiled=True)

    join_rows = lax.dynamic_index_in_dim(
        join_weight, jnp.clip(section - 4, 0, 3), 0, keepdims=False
    )

    high = lax.reduce_precision(ln_gain, 8, 7)
    middle = lax.reduce_precision(ln_gain - high, 8, 7)
    gain_parts = jnp.concatenate([high, middle, ln_gain - high - middle], axis=0).astype(
        jnp.bfloat16
    )

    def pack(half, gain_half):
        columns = HALF * half
        qkv = lax.dynamic_slice_in_dim(qkv_weight[0].reshape(12, 3, D), columns, HALF, 2)
        return jnp.concatenate(
            [
                qkv.transpose(1, 0, 2).reshape(36, HALF),
                lax.dynamic_slice_in_dim(out_weight[0], columns, HALF, 1),
                lax.dynamic_slice_in_dim(join_rows, columns, HALF, 1),
                lax.dynamic_slice_in_dim(gain_parts, HALF * gain_half, HALF, 1),
            ],
            axis=0,
        )

    own_pack, cross_pack, whole = lax.optimization_barrier(
        (pack(core, core), pack(1 - core, core), stream_in[0])
    )
    straight = lax.ppermute(own_pack, SECTION, onward)
    crossed = lax.ppermute(
        cross_pack,
        AXES,
        [
            (i, ((i // REPLICAS + 1) % SECTIONS) * REPLICAS + ((i % REPLICAS) ^ 1))
            for i in range(SECTIONS * REPLICAS)
        ],
    )
    gain_halves = [
        jnp.sum(part[72:].astype(jnp.float32), axis=0, keepdims=True) for part in (straight, crossed)
    ]
    gain_row = jnp.where(
        core == 0,
        jnp.concatenate(gain_halves, axis=1),
        jnp.concatenate(gain_halves[::-1], axis=1),
    )
    pair = jnp.concatenate([straight[:72], crossed[:72]], axis=0)
    places = jnp.where(core == 0, arrival_places(0), arrival_places(1))
    source = lax.broadcasted_iota(jnp.int32, (576, 576), 1)
    order = (source == places[:, None]).astype(jnp.bfloat16)
    order, pair = lax.optimization_barrier((order, pair))
    near = lax.all_gather(pair, "yl", axis=0, tiled=True)
    near = jnp.dot(
        order, near, preferred_element_type=jnp.float32
    ).astype(jnp.bfloat16)

    early = lax.ppermute(whole[:EARLY], SECTION, onward)
    moved = lax.ppermute(whole[DIRECT:], SECTION, [(1, 7), (2, 6), (3, 5)])

    near, part_direct, part_late, gain_row, moved, early = lax.optimization_barrier(
        (near, whole[:DIRECT], whole[EARLY:], gain_row, moved, early)
    )
    mine = lax.all_gather(near, "z", axis=0, tiled=False)
    late = lax.ppermute(part_late, SECTION, onward)
    direct = lax.ppermute(part_direct, SECTION, [(1, 0), (2, 7), (3, 6)])
    around = lax.ppermute(moved, SECTION, [(5, 6), (6, 7), (7, 0)])
    level = level.reshape(4, 2, 12, D)
    halves = [level[:, 0].reshape(48, D), level[:, 1].reshape(48, D)]
    level = jnp.where(core == 0, *halves) + lax.ppermute(
        jnp.where(core == 0, *halves[::-1]), "c", swap
    )
    level = level.reshape(4, 12, D)
    mine, direct, around, level = lax.optimization_barrier((mine, direct, around, level))
    other = [
        lax.ppermute(part, "c", swap) for part in jnp.split(mine, SWAPS, axis=0)
    ]

    times = time_rows(timestep).astype(jnp.float32).reshape(-1, 1, D)
    stream_out = run_block(place, times, gain_row, mine, other, early, late, direct, around)

    pieces = lax.all_to_all(level, "yl", 0, 0, tiled=True)
    stream_out, pieces = lax.optimization_barrier((stream_out, pieces))
    weight_grad = jnp.sum(pieces.reshape(4, 12, D), axis=0)
    return (stream_out[None], weight_grad[None])


def solution(mesh):
    fine = Mesh(mesh.devices.reshape(4, 2, 8, 4, 2), AXES)
    section, dp = ("x", "yh"), ("z", "yl", "c")
    return jax.shard_map(
        on_device,
        mesh=fine,
        in_specs=(
            P(section, dp, None),
            P(dp),
            P(section, None),
            P(section, dp, None),
            P(section, dp, None),
            P(None, dp, None),
            P(section, dp, None),
            P(section, dp, None),
        ),
        out_specs=(P(section, dp, None), P(section, dp, None)),
        check_vma=False,
    )
```

time: 173 us -> 164 us (0.948)
  the two profiles are of different devices: /device:TPU:196 before, /device:TPU:1 now
where the time goes in v3:
time: 164 us; the launch traced here: 163 us
  starting transfers between devices  50.1 us (31%)
  waiting for transfers between devices  42.1 us (26%)
  Pallas kernels  19.6 us (12%)
  blocking collectives  15.6 us (10%)
  between operations  14.4 us (9%)
  local copies, waits for them, and re-layouts  12.3 us (8%)
  matrix products  5.44 us (3%)
  other arithmetic  3.08 us (2%)
    all_gather x1, waiting for transfers between devices, on_device(): mine = lax.all_gather(near, 'z', axis=0, tiled=False)  20 us
    pallas_call x1, Pallas kernels, run_block(): pl.pallas_call(block_kernel, out_shape=jax.ShapeDtypeStruct((rows, D), jn...  19.6 us
    ppermute x1, waiting for transfers between devices, on_device(): around = lax.ppermute(moved, SECTION, [(5, 6), (6, 7), (7, 0)])  19.1 us
    all_gather x1, blocking collectives, on_device(): near = lax.all_gather(pair, 'yl', axis=0, tiled=True)  15.6 us
    ppermute x4, starting transfers between devices, on_device(): lax.ppermute(part, 'c', swap)  8.82 us
    ppermute x1, starting transfers between devices, on_device(): straight = lax.ppermute(own_pack, SECTION, onward)  8.28 us
    ppermute x1, starting transfers between devices, on_device(): early = lax.ppermute(whole[:EARLY], SECTION, onward)  7.44 us
    ppermute x1, starting transfers between devices, on_device(): late = lax.ppermute(part_late, SECTION, onward)  7.09 us
  transfers between devices with their start and end apart: 15, of which 4 were waited for; matrix products, arithmetic and copies ran while one was open for 9% of the time, Pallas kernels for 12%

profile of v3, /device:TPU:1, one launch (start us, length us, event | category | flops | bytes accessed | tf_op | source)
XLA Modules:
  0.0 162.8 jit_solution(2721418860880514247)
XLA Ops:
  7.2 1.2 copy-done
  8.4 4.1 %fusion.1 = f32[768,768]{1,0:T(8,128)} fusion(bf16[1,771,768]{2,1,0:T(8,128)(2,1)S(1)} %copy-done, bf16[1,771,768]{2,1,0:T(8,128)(2,1)} %param.16), kind=kOutput, calls=%fused_computation.3 | convolution fusion | flops 909508608 | bytes 4727808 | tf_op jit(solution)/shard_map/dot_general | solution.py:238
  12.7 0.8 copy-done.2
  13.7 0.9 dynamic-slice_bitcast_fusion
  14.7 8.3 %collective-permute-start = (bf16[75,384]{1,0:T(8,128)(2,1)S(1)}, bf16[75,384]{1,0:T(8,128)(2,1)}, u32[]{:S(2)}, u32[]{:S(2)}) collective-permute-start(bf16[75,384]{1,0:T(8,128)(2,1)S(1)} %get-tuple-element.19), channel_id=1, source_target_pairs={{0,64},{64,128},{128,192},{192,256},{256,320},{320,384},{384,448},... | collective-permute-start | bytes 172808 | tf_op jit(solution)/shard_map/ppermute | solution.py:269
  23.0 3.5 %collective-permute-start.1 = (bf16[75,384]{1,0:T(8,128)(2,1)S(1)}, bf16[75,384]{1,0:T(8,128)(2,1)S(1)}, u32[]{:S(2)}, u32[]{:S(2)}) collective-permute-start(bf16[75,384]{1,0:T(8,128)(2,1)S(1)} %get-tuple-element.20), channel_id=1, source_target_pairs={{0,65},{1,64},{2,67},{3,66},{4,69},{5,68},{6,71},{7,70},{8,73},{9,... | collective-permute-start | bytes 172808 | tf_op jit(solution)/shard_map/ppermute | solution.py:270
  26.5 0.8 slice.37
  27.3 7.4 %collective-permute-start.3 = (bf16[160,768]{1,0:T(8,128)(2,1)}, bf16[160,768]{1,0:T(8,128)(2,1)}, u32[]{:S(2)}, u32[]{:S(2)}) collective-permute-start(bf16[160,768]{1,0:T(8,128)(2,1)} %slice.37), channel_id=1, source_target_pairs={{0,64},{64,128},{128,192},{192,256},{256,320},{320,384},{384,448},... | collective-permute-start | bytes 737288 | tf_op jit(solution)/shard_map/ppermute | solution.py:296
  34.7 0.9 slice.36
  35.6 1.5 collective-permute-start.2
  37.3 0.9 slice.32
  38.2 0.8 slice.40
  39.1 0.7 convert_reduce_fusion.1
  40.4 15.6 %all_gather.9 = bf16[576,384]{1,0:T(8,128)(2,1)S(1)} all-gather(bf16[144,384]{1,0:T(8,128)(2,1)S(1)} %pad_maximum_fusion), channel_id=1, replica_groups=mesh['x'=4,'yh'=2,'z'=8,'yl'=4,'c'=2] {'yl'}, dimensions={0}, use_global_device_ids=true | all-gather | bytes 552960 | tf_op jit(solution)/shard_map/all_gather | solution.py:291
  56.0 1.3 convolution_convert_fusion
  57.4 1.3 collective-permute-start.5
  58.7 1.3 collective-permute-start.4
  60.0 1.0 reduce-scatter.2.cloned.1.call-done
  61.0 1.0 reshape.185
  62.1 6.5 %collective-permute-start.6 = (f32[48,768]{1,0:T(8,128)S(1)}, f32[48,768]{1,0:T(8,128)S(1)}, u32[]{:S(2)}, u32[]{:S(2)}) collective-permute-start(f32[48,768]{1,0:T(8,128)S(1)} %select_n.72), channel_id=1, source_target_pairs={{0,1},{1,0},{2,3},{3,2},{4,5},{5,4},{6,7},{7,6},{8,9},{9,8},{10,11... | collective-permute-start | bytes 442376 | tf_op jit(solution)/shard_map/ppermute | solution.py:308
  68.5 7.1 %collective-permute-start.11 = (bf16[611,768]{1,0:T(8,128)(2,1)S(1)}, bf16[611,768]{1,0:T(8,128)(2,1)}, u32[]{:S(2)}, u32[]{:S(2)}) collective-permute-start(bf16[611,768]{1,0:T(8,128)(2,1)S(1)} %slice.33), channel_id=1, source_target_pairs={{0,64},{64,128},{128,192},{192,256},{256,320},{320,384},{384,448},... | collective-permute-start | bytes 2815496 | tf_op jit(solution)/shard_map/ppermute | solution.py:303
  75.7 0.7 reshape.186
  76.4 2.0 %collective-permute-done.4.refs_6_ = bf16[384,768]{1,0:T(8,128)(2,1)} collective-permute-done((bf16[384,768]{1,0:T(8,128)(2,1)}, bf16[384,768]{1,0:T(8,128)(2,1)}, u32[]{:S(2)}, u32[]{:S(2)}) %collective-permute-start.4) | collective-permute-done | bytes 589856 | tf_op jit(solution)/shard_map/ppermute | solution.py:304
  78.3 19.1 %collective-permute-done.5.refs_7_ = bf16[387,768]{1,0:T(8,128)(2,1)} collective-permute-done((bf16[387,768]{1,0:T(8,128)(2,1)}, bf16[387,768]{1,0:T(8,128)(2,1)}, u32[]{:S(2)}, u32[]{:S(2)}) %collective-permute-start.5) | collective-permute-done | bytes 594464 | tf_op jit(solution)/shard_map/ppermute | solution.py:305
  97.4 20.0 %all-gather.3.cloned.1.call-done = bf16[4608,384]{1,0:T(8,128)(2,1)} async-done(((bf16[576,384]{1,0:T(8,128)(2,1)}), bf16[4608,384]{1,0:T(8,128)(2,1)}) %all-gather.3.cloned.1.call-update) | async-done | bytes 3538960 | tf_op jit(solution)/shard_map/all_gather | solution.py:302
  117.4 3.6 %fusion.11 = (bf16[2,576,384]{2,1,0:T(8,128)(2,1)}, bf16[2,576,384]{2,1,0:T(8,128)(2,1)}, bf16[2,576,384]{2,1,0:T(8,128)(2,1)}, bf16[2,576,384]{2,1,0:T(8,128)(2,1)S(1)}) fusion(bf16[8,576,384]{2,1,0:T(8,128)(2,1)} %bitcast.33), kind=kLoop, calls=%fused_computation.42 | loop fusion | bytes 7077888 | tf_op jit(solution)/shard_map/split | solution.py:314
  121.0 2.6 %collective-permute-start.10 = (bf16[2,576,384]{2,1,0:T(8,128)(2,1)}, bf16[2,576,384]{2,1,0:T(8,128)(2,1)}, u32[]{:S(2)}, u32[]{:S(2)}) collective-permute-start(bf16[2,576,384]{2,1,0:T(8,128)(2,1)} %get-tuple-element.36), channel_id=1, source_target_pairs={{0,1},{1,0},{2,3},{3,2},{4,5},{5,4},{6,7},{7,6},{8,9},{9,8},{10,11... | collective-permute-start | bytes 2654216 | tf_op jit(solution)/shard_map/ppermute | solution.py:314
  123.6 1.9 %collective-permute-start.9 = (bf16[2,576,384]{2,1,0:T(8,128)(2,1)}, bf16[2,576,384]{2,1,0:T(8,128)(2,1)}, u32[]{:S(2)}, u32[]{:S(2)}) collective-permute-start(bf16[2,576,384]{2,1,0:T(8,128)(2,1)} %get-tuple-element.37), channel_id=1, source_target_pairs={{0,1},{1,0},{2,3},{3,2},{4,5},{5,4},{6,7},{7,6},{8,9},{9,8},{10,11... | collective-permute-start | bytes 2654216 | tf_op jit(solution)/shard_map/ppermute | solution.py:314
  125.5 2.4 %collective-permute-start.8 = (bf16[2,576,384]{2,1,0:T(8,128)(2,1)}, bf16[2,576,384]{2,1,0:T(8,128)(2,1)}, u32[]{:S(2)}, u32[]{:S(2)}) collective-permute-start(bf16[2,576,384]{2,1,0:T(8,128)(2,1)} %get-tuple-element.38), channel_id=1, source_target_pairs={{0,1},{1,0},{2,3},{3,2},{4,5},{5,4},{6,7},{7,6},{8,9},{9,8},{10,11... | collective-permute-start | bytes 2654216 | tf_op jit(solution)/shard_map/ppermute | solution.py:314
  127.9 1.9 %collective-permute-start.7 = (bf16[2,576,384]{2,1,0:T(8,128)(2,1)S(1)}, bf16[2,576,384]{2,1,0:T(8,128)(2,1)}, u32[]{:S(2)}, u32[]{:S(2)}) collective-permute-start(bf16[2,576,384]{2,1,0:T(8,128)(2,1)S(1)} %get-tuple-element.39), channel_id=1, source_target_pairs={{0,1},{1,0},{2,3},{3,2},{4,5},{5,4},{6,7},{7,6},{8,9},{9,8},{10,11... | collective-permute-start | bytes 2654216 | tf_op jit(solution)/shard_map/ppermute | solution.py:314
  131.3 4.3 %all-to-all-start = ((f32[4,12,768]{2,1,0:T(8,128)}), f32[4,12,768]{2,1,0:T(8,128)S(1)}, u32[]{:S(2)}, u32[]{:S(2)}) async-start(f32[4,12,768]{2,1,0:T(8,128)} %reshape.186), calls=%async_computation.1 | async-start | bytes 393216 | tf_op jit(solution)/shard_map/all_to_all | solution.py:320
  135.6 19.6 %shard_map.113 = bf16[771,768]{1,0:T(8,128)(2,1)} custom-call(s32[2]{0:T(128)} %pad_add_fusion.place_ref, f32[3,1,768]{2,1,0:T(1,128)} %maximum_convert_fusion.time_ref, f32[1,768]{1,0:T(1,128)} %broadcast_select_fusion.gain_ref, bf16[8,576,384]{2,1,0:T(8,128)(2,1)} %bitcast.34, bf16[2,576,384]{2,1,0:T(8,128)(2,1)} %collective-permute-done.7.refs_0_, ...), custom_call_target="tpu_custom_call" | custom-call | flops 6366560256 | bytes 12582912 | tf_op jit(solution)/shard_map/pallas_call | solution.py:192
  (60 shorter events, 3.4 us)
Async XLA Ops:
  7.2 1.3 copy-start
  7.2 53.8 %reduce-scatter.2.cloned.1.call-start = ((), (), s32[]{:S(2)}) async-start(), calls=%async_computation.2 | async-start | bytes 2654208 | tf_op jit(solution)/shard_map/reduce_scatter | solution.py:241
  12.6 0.9 copy-start.2
  12.6 1.0 copy-start.6
  12.6 1.2 copy-start.3
  12.6 13.9 %copy-start.1 = (bf16[1,771,768]{2,1,0:T(8,128)(2,1)S(1)}, bf16[1,771,768]{2,1,0:T(8,128)(2,1)}, u32[]{:S(2)}) copy-start(bf16[1,771,768]{2,1,0:T(8,128)(2,1)} %param.10) | copy-start | bytes 3552772
  12.6 104.8 %all-gather.3.cloned.1.call-start = ((), (), s32[]{:S(2)}) async-start(), calls=%async_computation.3 | async-start | bytes 3981312 | tf_op jit(solution)/shard_map/all_gather | solution.py:302
  13.5 23.5 %copy-start.4 = (s32[576]{0:T(1024)S(1)}, s32[576]{0:T(1024)}, u32[]{:S(2)}) copy-start(s32[576]{0:T(1024)} %constant.80.clone) | copy-start | bytes 6916
  13.5 23.5 %copy-start.5 = (s32[576]{0:T(1024)S(1)}, s32[576]{0:T(1024)}, u32[]{:S(2)}) copy-start(s32[576]{0:T(1024)} %constant.79.clone) | copy-start | bytes 6916
  14.7 23.5 %collective-permute-start = (bf16[75,384]{1,0:T(8,128)(2,1)S(1)}, bf16[75,384]{1,0:T(8,128)(2,1)}, u32[]{:S(2)}, u32[]{:S(2)}) collective-permute-start(bf16[75,384]{1,0:T(8,128)(2,1)S(1)} %get-tuple-element.19), channel_id=1, source_target_pairs={{0,64},{64,128},{128,192},{192,256},{256,320},{320,384},{384,448},... | collective-permute-start | bytes 172808 | tf_op jit(solution)/shard_map/ppermute | solution.py:269
  23.0 16.1 %collective-permute-start.1 = (bf16[75,384]{1,0:T(8,128)(2,1)S(1)}, bf16[75,384]{1,0:T(8,128)(2,1)S(1)}, u32[]{:S(2)}, u32[]{:S(2)}) collective-permute-start(bf16[75,384]{1,0:T(8,128)(2,1)S(1)} %get-tuple-element.20), channel_id=1, source_target_pairs={{0,65},{1,64},{2,67},{3,66},{4,69},{5,68},{6,71},{7,70},{8,73},{9,... | collective-permute-start | bytes 172808 | tf_op jit(solution)/shard_map/ppermute | solution.py:270
  27.3 30.1 %collective-permute-start.3 = (bf16[160,768]{1,0:T(8,128)(2,1)}, bf16[160,768]{1,0:T(8,128)(2,1)}, u32[]{:S(2)}, u32[]{:S(2)}) collective-permute-start(bf16[160,768]{1,0:T(8,128)(2,1)} %slice.37), channel_id=1, source_target_pairs={{0,64},{64,128},{128,192},{192,256},{256,320},{320,384},{384,448},... | collective-permute-start | bytes 737288 | tf_op jit(solution)/shard_map/ppermute | solution.py:296
  35.6 21.8 %collective-permute-start.2 = (bf16[387,768]{1,0:T(8,128)(2,1)}, bf16[387,768]{1,0:T(8,128)(2,1)}, u32[]{:S(2)}, u32[]{:S(2)}) collective-permute-start(bf16[387,768]{1,0:T(8,128)(2,1)} %slice.36), channel_id=1, source_target_pairs={{64,448},{128,384},{192,320},{65,449},{129,385},{193,321},{66,450}... | collective-permute-start | bytes 1783304 | tf_op jit(solution)/shard_map/ppermute | solution.py:297
  57.4 40.1 %collective-permute-start.5 = (bf16[387,768]{1,0:T(8,128)(2,1)}, bf16[387,768]{1,0:T(8,128)(2,1)}, u32[]{:S(2)}, u32[]{:S(2)}) collective-permute-start(bf16[387,768]{1,0:T(8,128)(2,1)} %collective-permute-done.2), channel_id=1, source_target_pairs={{320,384},{384,448},{448,0},{321,385},{385,449},{449,1},{322,386},... | collective-permute-start | bytes 1783304 | tf_op jit(solution)/shard_map/ppermute | solution.py:305
  58.7 19.7 %collective-permute-start.4 = (bf16[384,768]{1,0:T(8,128)(2,1)}, bf16[384,768]{1,0:T(8,128)(2,1)}, u32[]{:S(2)}, u32[]{:S(2)}) collective-permute-start(bf16[384,768]{1,0:T(8,128)(2,1)} %slice.32), channel_id=1, source_target_pairs={{64,0},{128,448},{192,384},{65,1},{129,449},{193,385},{66,2},{130,... | collective-permute-start | bytes 1769480 | tf_op jit(solution)/shard_map/ppermute | solution.py:304
  62.1 13.6 %collective-permute-start.6 = (f32[48,768]{1,0:T(8,128)S(1)}, f32[48,768]{1,0:T(8,128)S(1)}, u32[]{:S(2)}, u32[]{:S(2)}) collective-permute-start(f32[48,768]{1,0:T(8,128)S(1)} %select_n.72), channel_id=1, source_target_pairs={{0,1},{1,0},{2,3},{3,2},{4,5},{5,4},{6,7},{7,6},{8,9},{9,8},{10,11... | collective-permute-start | bytes 442376 | tf_op jit(solution)/shard_map/ppermute | solution.py:308
  68.5 67.1 %collective-permute-start.11 = (bf16[611,768]{1,0:T(8,128)(2,1)S(1)}, bf16[611,768]{1,0:T(8,128)(2,1)}, u32[]{:S(2)}, u32[]{:S(2)}) collective-permute-start(bf16[611,768]{1,0:T(8,128)(2,1)S(1)} %slice.33), channel_id=1, source_target_pairs={{0,64},{64,128},{128,192},{192,256},{256,320},{320,384},{384,448},... | collective-permute-start | bytes 2815496 | tf_op jit(solution)/shard_map/ppermute | solution.py:303
  117.4 12.4 %copy-start.7 = (s32[3]{0:T(128)S(1)}, s32[3]{0:T(128)}, u32[]{:S(2)}) copy-start(s32[3]{0:T(128)} %param.11) | copy-start | bytes 40
  121.0 14.6 %collective-permute-start.10 = (bf16[2,576,384]{2,1,0:T(8,128)(2,1)}, bf16[2,576,384]{2,1,0:T(8,128)(2,1)}, u32[]{:S(2)}, u32[]{:S(2)}) collective-permute-start(bf16[2,576,384]{2,1,0:T(8,128)(2,1)} %get-tuple-element.36), channel_id=1, source_target_pairs={{0,1},{1,0},{2,3},{3,2},{4,5},{5,4},{6,7},{7,6},{8,9},{9,8},{10,11... | collective-permute-start | bytes 2654216 | tf_op jit(solution)/shard_map/ppermute | solution.py:314
  123.6 12.0 %collective-permute-start.9 = (bf16[2,576,384]{2,1,0:T(8,128)(2,1)}, bf16[2,576,384]{2,1,0:T(8,128)(2,1)}, u32[]{:S(2)}, u32[]{:S(2)}) collective-permute-start(bf16[2,576,384]{2,1,0:T(8,128)(2,1)} %get-tuple-element.37), channel_id=1, source_target_pairs={{0,1},{1,0},{2,3},{3,2},{4,5},{5,4},{6,7},{7,6},{8,9},{9,8},{10,11... | collective-permute-start | bytes 2654216 | tf_op jit(solution)/shard_map/ppermute | solution.py:314
  125.5 10.1 %collective-permute-start.8 = (bf16[2,576,384]{2,1,0:T(8,128)(2,1)}, bf16[2,576,384]{2,1,0:T(8,128)(2,1)}, u32[]{:S(2)}, u32[]{:S(2)}) collective-permute-start(bf16[2,576,384]{2,1,0:T(8,128)(2,1)} %get-tuple-element.38), channel_id=1, source_target_pairs={{0,1},{1,0},{2,3},{3,2},{4,5},{5,4},{6,7},{7,6},{8,9},{9,8},{10,11... | collective-permute-start | bytes 2654216 | tf_op jit(solution)/shard_map/ppermute | solution.py:314
  127.9 7.7 %collective-permute-start.7 = (bf16[2,576,384]{2,1,0:T(8,128)(2,1)S(1)}, bf16[2,576,384]{2,1,0:T(8,128)(2,1)}, u32[]{:S(2)}, u32[]{:S(2)}) collective-permute-start(bf16[2,576,384]{2,1,0:T(8,128)(2,1)S(1)} %get-tuple-element.39), channel_id=1, source_target_pairs={{0,1},{1,0},{2,3},{3,2},{4,5},{5,4},{6,7},{7,6},{8,9},{9,8},{10,11... | collective-permute-start | bytes 2654216 | tf_op jit(solution)/shard_map/ppermute | solution.py:314
  131.3 24.0 %all-to-all-start = ((f32[4,12,768]{2,1,0:T(8,128)}), f32[4,12,768]{2,1,0:T(8,128)S(1)}, u32[]{:S(2)}, u32[]{:S(2)}) async-start(f32[4,12,768]{2,1,0:T(8,128)} %reshape.186), calls=%async_computation.1 | async-start | bytes 393216 | tf_op jit(solution)/shard_map/all_to_all | solution.py:320
Sparse Core Ops, SparseCore 0:
  12.7 48.2 reduce-scatter.1
  63.1 54.3 all-gather.2

commit v4 on v3

--- a/solution.py
+++ b/solution.py
@@ -16,7 +16,7 @@
 PAD = 272
 KEYS = 384
 HALF = D // 2
-EARLY = 160
+EARLY = 176
 DIRECT = 384
 SWAPS = 4
 SECTIONS = 8
@@ -63,7 +63,8 @@
 def block_kernel(place_ref, time_ref, gain_ref, mine, *refs):
     other, refs = refs[:SWAPS], refs[SWAPS:]
     early, late, direct, around, out_ref, *refs = refs
-    held, entering, skip, block_in, normed, qkv_rows, image_context, context, sems = refs
+    held, entering, skip, block_in, normed, qkv_rows, image_context, context, *refs = refs
+    scores_ref, powered_ref, sems = refs
     join_copies, qkv_copies, out_copies = weight_copies(mine, other, held, sems)
     for copy in join_copies + qkv_copies + out_copies:
         copy.start()
@@ -155,13 +156,17 @@
                     (((1,), (1,)), ((), ())),
                     preferred_element_type=jnp.float32,
                 )
-                main, last = scores[:, :256], jnp.where(real, scores[:, 256:], -1e30)
-                widest = jnp.maximum(jnp.maximum(main[:, :128], main[:, 128:]), last)
-                row_max = jnp.max(widest, axis=-1, keepdims=True)
                 factor = HEAD_DIM ** (-0.5) * math.log2(math.e)
-                powered = jnp.concatenate(
-                    [jnp.exp2((main - row_max) * factor), jnp.exp2((last - row_max) * factor)], axis=1
-                ).astype(jnp.bfloat16)
+                scores_ref[...] = scores
+                for first, size in ((0, 128), (128, 128), (256, 16)):
+                    rows = slice(first, first + size)
+                    main = scores_ref[rows, :256]
+                    last = jnp.where(real[:size], scores_ref[rows, 256:], -1e30)
+                    widest = jnp.maximum(jnp.maximum(main[:, :128], main[:, 128:]), last)
+                    row_max = jnp.max(widest, axis=-1, keepdims=True)
+                    powered_ref[rows, :256] = jnp.exp2((main - row_max) * factor).astype(jnp.bfloat16)
+                    powered_ref[rows, 256:] = jnp.exp2((last - row_max) * factor).astype(jnp.bfloat16)
+                powered = powered_ref[...]
                 sums.append(
                     jnp.dot(powered, jnp.where(here_k, values, one), preferred_element_type=jnp.float32)
                 )
@@ -206,6 +211,8 @@
             pltpu.VMEM((images, KEYS, 3 * D), jnp.bfloat16),
             pltpu.VMEM((images, PAD, D), jnp.bfloat16),
             pltpu.VMEM((rows, D), jnp.bfloat16),
+            pltpu.VMEM((PAD, KEYS), jnp.float32),
+            pltpu.VMEM((PAD, KEYS), jnp.bfloat16),
             pltpu.SemaphoreType.DMA((len(GROUPS) * (1 + SWAPS),)),
         ],
         compiler_params=pltpu.CompilerParams(vmem_limit_bytes=57 * 2**20),

time: 164 us -> 165 us (level)
  blocking collectives: 15.6 us -> 18.8 us
    all_gather x1, blocking collectives: 15.6 us -> 18.8 us  [on_device(): near = lax.all_gather(pair, 'yl', axis=0, tiled=True)]
    ppermute x1, waiting for transfers between devices: 1.97 us -> 3.75 us  [on_device(): direct = lax.ppermute(part_direct, SECTION, [(1, 0), (2, 7), (3, 6)])]
  transfers between devices with their start and end apart: 15 -> 15, of which waited for: 4 -> 3; matrix products, arithmetic and copies ran while one was open for 9% -> 8% of each run, Pallas kernels for 12% -> 12%
where the time goes in v4:
time: 165 us; the launch traced here: 163 us
  starting transfers between devices  49.4 us (30%)
  waiting for transfers between devices  41.2 us (25%)
  Pallas kernels  19.6 us (12%)
  blocking collectives  18.8 us (11%)
  between operations  14.5 us (9%)
  local copies, waits for them, and re-layouts  11.5 us (7%)
  matrix products  5.44 us (3%)
  other arithmetic  2.34 us (1%)
    pallas_call x1, Pallas kernels, run_block(): pl.pallas_call(block_kernel, out_shape=jax.ShapeDtypeStruct((rows, D), jn...  19.6 us
    all_gather x1, blocking collectives, on_device(): near = lax.all_gather(pair, 'yl', axis=0, tiled=True)  18.8 us
    all_gather x1, waiting for transfers between devices, on_device(): mine = lax.all_gather(near, 'z', axis=0, tiled=False)  18.8 us
    ppermute x1, waiting for transfers between devices, on_device(): around = lax.ppermute(moved, SECTION, [(5, 6), (6, 7), (7, 0)])  18.5 us
    ppermute x4, starting transfers between devices, on_device(): lax.ppermute(part, 'c', swap)  8.82 us
    ppermute x1, starting transfers between devices, on_device(): straight = lax.ppermute(own_pack, SECTION, onward)  8.28 us
    ppermute x1, starting transfers between devices, on_device(): early = lax.ppermute(whole[:EARLY], SECTION, onward)  7.44 us
    ppermute x1, starting transfers between devices, on_device(): late = lax.ppermute(part_late, SECTION, onward)  7.09 us
  transfers between devices with their start and end apart: 15, of which 3 were waited for; matrix products, arithmetic and copies ran while one was open for 8% of the time, Pallas kernels for 12%

profile of v4, /device:TPU:1, one launch (start us, length us, event | category | flops | bytes accessed | tf_op | source)
XLA Modules:
  0.0 162.7 jit_solution(15518228574941237983)
XLA Ops:
  7.2 1.2 copy-done
  8.4 4.1 %fusion.1 = f32[768,768]{1,0:T(8,128)} fusion(bf16[1,771,768]{2,1,0:T(8,128)(2,1)S(1)} %copy-done, bf16[1,771,768]{2,1,0:T(8,128)(2,1)} %param.16), kind=kOutput, calls=%fused_computation.3 | convolution fusion | flops 909508608 | bytes 4727808 | tf_op jit(solution)/shard_map/dot_general | solution.py:245
  12.7 0.8 copy-done.2
  13.7 0.9 dynamic-slice_bitcast_fusion
  14.7 8.3 %collective-permute-start = (bf16[75,384]{1,0:T(8,128)(2,1)S(1)}, bf16[75,384]{1,0:T(8,128)(2,1)S(1)}, u32[]{:S(2)}, u32[]{:S(2)}) collective-permute-start(bf16[75,384]{1,0:T(8,128)(2,1)S(1)} %get-tuple-element.19), channel_id=1, source_target_pairs={{0,64},{64,128},{128,192},{192,256},{256,320},{320,384},{384,448},... | collective-permute-start | bytes 172808 | tf_op jit(solution)/shard_map/ppermute | solution.py:276
  23.0 3.5 %collective-permute-start.1 = (bf16[75,384]{1,0:T(8,128)(2,1)S(1)}, bf16[75,384]{1,0:T(8,128)(2,1)S(1)}, u32[]{:S(2)}, u32[]{:S(2)}) collective-permute-start(bf16[75,384]{1,0:T(8,128)(2,1)S(1)} %get-tuple-element.20), channel_id=1, source_target_pairs={{0,65},{1,64},{2,67},{3,66},{4,69},{5,68},{6,71},{7,70},{8,73},{9,... | collective-permute-start | bytes 172808 | tf_op jit(solution)/shard_map/ppermute | solution.py:277
  26.5 0.8 slice.37
  27.3 7.4 %collective-permute-start.3 = (bf16[176,768]{1,0:T(8,128)(2,1)}, bf16[176,768]{1,0:T(8,128)(2,1)}, u32[]{:S(2)}, u32[]{:S(2)}) collective-permute-start(bf16[176,768]{1,0:T(8,128)(2,1)} %slice.37), channel_id=1, source_target_pairs={{0,64},{64,128},{128,192},{192,256},{256,320},{320,384},{384,448},... | collective-permute-start | bytes 811016 | tf_op jit(solution)/shard_map/ppermute | solution.py:303
  34.7 0.9 slice.36
  35.6 1.5 collective-permute-start.2
  37.3 0.9 slice.32
  38.3 18.8 %all_gather.9 = bf16[576,384]{1,0:T(8,128)(2,1)S(1)} all-gather(bf16[144,384]{1,0:T(8,128)(2,1)S(1)} %pad_maximum_fusion), channel_id=1, replica_groups=mesh['x'=4,'yh'=2,'z'=8,'yl'=4,'c'=2] {'yl'}, dimensions={0}, use_global_device_ids=true | all-gather | bytes 552960 | tf_op jit(solution)/shard_map/all_gather | solution.py:298
  57.1 0.6 broadcast_select_fusion.gain_ref
  57.7 1.3 convolution_convert_fusion
  59.1 1.3 collective-permute-start.5
  60.4 1.3 collective-permute-start.4
  61.7 1.0 reshape.185
  62.8 5.7 %collective-permute-start.6 = (f32[48,768]{1,0:T(8,128)S(1)}, f32[48,768]{1,0:T(8,128)S(1)}, u32[]{:S(2)}, u32[]{:S(2)}) collective-permute-start(f32[48,768]{1,0:T(8,128)S(1)} %select_n.72), channel_id=1, source_target_pairs={{0,1},{1,0},{2,3},{3,2},{4,5},{5,4},{6,7},{7,6},{8,9},{9,8},{10,11... | collective-permute-start | bytes 442376 | tf_op jit(solution)/shard_map/ppermute | solution.py:315
  68.5 7.1 %collective-permute-start.11 = (bf16[595,768]{1,0:T(8,128)(2,1)S(1)}, bf16[595,768]{1,0:T(8,128)(2,1)}, u32[]{:S(2)}, u32[]{:S(2)}) collective-permute-start(bf16[595,768]{1,0:T(8,128)(2,1)S(1)} %slice.33), channel_id=1, source_target_pairs={{0,64},{64,128},{128,192},{192,256},{256,320},{320,384},{384,448},... | collective-permute-start | bytes 2741768 | tf_op jit(solution)/shard_map/ppermute | solution.py:310
  75.7 0.7 reshape.186
  76.4 3.8 %collective-permute-done.4.refs_6_ = bf16[384,768]{1,0:T(8,128)(2,1)} collective-permute-done((bf16[384,768]{1,0:T(8,128)(2,1)}, bf16[384,768]{1,0:T(8,128)(2,1)}, u32[]{:S(2)}, u32[]{:S(2)}) %collective-permute-start.4) | collective-permute-done | bytes 589856 | tf_op jit(solution)/shard_map/ppermute | solution.py:311
  80.1 18.5 %collective-permute-done.5.refs_7_ = bf16[387,768]{1,0:T(8,128)(2,1)} collective-permute-done((bf16[387,768]{1,0:T(8,128)(2,1)}, bf16[387,768]{1,0:T(8,128)(2,1)}, u32[]{:S(2)}, u32[]{:S(2)}) %collective-permute-start.5) | collective-permute-done | bytes 594464 | tf_op jit(solution)/shard_map/ppermute | solution.py:312
  98.6 18.8 %all-gather.3.cloned.1.call-done = bf16[4608,384]{1,0:T(8,128)(2,1)} async-done(((bf16[576,384]{1,0:T(8,128)(2,1)}), bf16[4608,384]{1,0:T(8,128)(2,1)}) %all-gather.3.cloned.1.call-update) | async-done | bytes 3538960 | tf_op jit(solution)/shard_map/all_gather | solution.py:309
  117.4 3.6 %fusion.11 = (bf16[2,576,384]{2,1,0:T(8,128)(2,1)}, bf16[2,576,384]{2,1,0:T(8,128)(2,1)}, bf16[2,576,384]{2,1,0:T(8,128)(2,1)}, bf16[2,576,384]{2,1,0:T(8,128)(2,1)S(1)}) fusion(bf16[8,576,384]{2,1,0:T(8,128)(2,1)} %bitcast.33), kind=kLoop, calls=%fused_computation.42 | loop fusion | bytes 7077888 | tf_op jit(solution)/shard_map/split | solution.py:321
  121.0 2.6 %collective-permute-start.10 = (bf16[2,576,384]{2,1,0:T(8,128)(2,1)}, bf16[2,576,384]{2,1,0:T(8,128)(2,1)}, u32[]{:S(2)}, u32[]{:S(2)}) collective-permute-start(bf16[2,576,384]{2,1,0:T(8,128)(2,1)} %get-tuple-element.36), channel_id=1, source_target_pairs={{0,1},{1,0},{2,3},{3,2},{4,5},{5,4},{6,7},{7,6},{8,9},{9,8},{10,11... | collective-permute-start | bytes 2654216 | tf_op jit(solution)/shard_map/ppermute | solution.py:321
  123.6 1.9 %collective-permute-start.9 = (bf16[2,576,384]{2,1,0:T(8,128)(2,1)}, bf16[2,576,384]{2,1,0:T(8,128)(2,1)}, u32[]{:S(2)}, u32[]{:S(2)}) collective-permute-start(bf16[2,576,384]{2,1,0:T(8,128)(2,1)} %get-tuple-element.37), channel_id=1, source_target_pairs={{0,1},{1,0},{2,3},{3,2},{4,5},{5,4},{6,7},{7,6},{8,9},{9,8},{10,11... | collective-permute-start | bytes 2654216 | tf_op jit(solution)/shard_map/ppermute | solution.py:321
  125.5 2.4 %collective-permute-start.8 = (bf16[2,576,384]{2,1,0:T(8,128)(2,1)}, bf16[2,576,384]{2,1,0:T(8,128)(2,1)}, u32[]{:S(2)}, u32[]{:S(2)}) collective-permute-start(bf16[2,576,384]{2,1,0:T(8,128)(2,1)} %get-tuple-element.38), channel_id=1, source_target_pairs={{0,1},{1,0},{2,3},{3,2},{4,5},{5,4},{6,7},{7,6},{8,9},{9,8},{10,11... | collective-permute-start | bytes 2654216 | tf_op jit(solution)/shard_map/ppermute | solution.py:321
  127.9 1.9 %collective-permute-start.7 = (bf16[2,576,384]{2,1,0:T(8,128)(2,1)S(1)}, bf16[2,576,384]{2,1,0:T(8,128)(2,1)}, u32[]{:S(2)}, u32[]{:S(2)}) collective-permute-start(bf16[2,576,384]{2,1,0:T(8,128)(2,1)S(1)} %get-tuple-element.39), channel_id=1, source_target_pairs={{0,1},{1,0},{2,3},{3,2},{4,5},{5,4},{6,7},{7,6},{8,9},{9,8},{10,11... | collective-permute-start | bytes 2654216 | tf_op jit(solution)/shard_map/ppermute | solution.py:321
  130.6 0.6 maximum_convert_fusion.time_ref
  131.2 4.3 %all-to-all-start = ((f32[4,12,768]{2,1,0:T(8,128)}), f32[4,12,768]{2,1,0:T(8,128)S(1)}, u32[]{:S(2)}, u32[]{:S(2)}) async-start(f32[4,12,768]{2,1,0:T(8,128)} %reshape.186), calls=%async_computation.1 | async-start | bytes 393216 | tf_op jit(solution)/shard_map/all_to_all | solution.py:327
  135.6 19.6 %shard_map.113 = bf16[771,768]{1,0:T(8,128)(2,1)} custom-call(s32[2]{0:T(128)} %pad_add_fusion.place_ref, f32[3,1,768]{2,1,0:T(1,128)} %maximum_convert_fusion.time_ref, f32[1,768]{1,0:T(1,128)} %broadcast_select_fusion.gain_ref, bf16[8,576,384]{2,1,0:T(8,128)(2,1)} %bitcast.34, bf16[2,576,384]{2,1,0:T(8,128)(2,1)} %collective-permute-done.7.refs_0_, ...), custom_call_target="tpu_custom_call" | custom-call | flops 6366560256 | bytes 12582912 | tf_op jit(solution)/shard_map/pallas_call | solution.py:197
  155.2 0.6 broadcast_in_dim.5
  (60 shorter events, 1.6 us)
Async XLA Ops:
  7.2 1.3 copy-start
  7.2 54.5 %reduce-scatter.2.cloned.1.call-start = ((), (), s32[]{:S(2)}) async-start(), calls=%async_computation.2 | async-start | bytes 2654208 | tf_op jit(solution)/shard_map/reduce_scatter | solution.py:248
  12.6 0.9 copy-start.2
  12.6 1.0 copy-start.6
  12.6 1.2 copy-start.3
  12.6 13.9 %copy-start.1 = (bf16[1,771,768]{2,1,0:T(8,128)(2,1)S(1)}, bf16[1,771,768]{2,1,0:T(8,128)(2,1)}, u32[]{:S(2)}) copy-start(bf16[1,771,768]{2,1,0:T(8,128)(2,1)} %param.10) | copy-start | bytes 3552772
  12.6 104.8 %all-gather.3.cloned.1.call-start = ((), (), s32[]{:S(2)}) async-start(), calls=%async_computation.3 | async-start | bytes 3981312 | tf_op jit(solution)/shard_map/all_gather | solution.py:309
  13.5 23.5 %copy-start.4 = (s32[576]{0:T(1024)S(1)}, s32[576]{0:T(1024)}, u32[]{:S(2)}) copy-start(s32[576]{0:T(1024)} %constant.80.clone) | copy-start | bytes 6916
  13.5 23.5 %copy-start.5 = (s32[576]{0:T(1024)S(1)}, s32[576]{0:T(1024)}, u32[]{:S(2)}) copy-start(s32[576]{0:T(1024)} %constant.79.clone) | copy-start | bytes 6916
  14.7 23.5 %collective-permute-start = (bf16[75,384]{1,0:T(8,128)(2,1)S(1)}, bf16[75,384]{1,0:T(8,128)(2,1)S(1)}, u32[]{:S(2)}, u32[]{:S(2)}) collective-permute-start(bf16[75,384]{1,0:T(8,128)(2,1)S(1)} %get-tuple-element.19), channel_id=1, source_target_pairs={{0,64},{64,128},{128,192},{192,256},{256,320},{320,384},{384,448},... | collective-permute-start | bytes 172808 | tf_op jit(solution)/shard_map/ppermute | solution.py:276
  23.0 15.3 %collective-permute-start.1 = (bf16[75,384]{1,0:T(8,128)(2,1)S(1)}, bf16[75,384]{1,0:T(8,128)(2,1)S(1)}, u32[]{:S(2)}, u32[]{:S(2)}) collective-permute-start(bf16[75,384]{1,0:T(8,128)(2,1)S(1)} %get-tuple-element.20), channel_id=1, source_target_pairs={{0,65},{1,64},{2,67},{3,66},{4,69},{5,68},{6,71},{7,70},{8,73},{9,... | collective-permute-start | bytes 172808 | tf_op jit(solution)/shard_map/ppermute | solution.py:277
  27.3 31.8 %collective-permute-start.3 = (bf16[176,768]{1,0:T(8,128)(2,1)}, bf16[176,768]{1,0:T(8,128)(2,1)}, u32[]{:S(2)}, u32[]{:S(2)}) collective-permute-start(bf16[176,768]{1,0:T(8,128)(2,1)} %slice.37), channel_id=1, source_target_pairs={{0,64},{64,128},{128,192},{192,256},{256,320},{320,384},{384,448},... | collective-permute-start | bytes 811016 | tf_op jit(solution)/shard_map/ppermute | solution.py:303
  35.6 23.5 %collective-permute-start.2 = (bf16[387,768]{1,0:T(8,128)(2,1)}, bf16[387,768]{1,0:T(8,128)(2,1)}, u32[]{:S(2)}, u32[]{:S(2)}) collective-permute-start(bf16[387,768]{1,0:T(8,128)(2,1)} %slice.36), channel_id=1, source_target_pairs={{64,448},{128,384},{192,320},{65,449},{129,385},{193,321},{66,450}... | collective-permute-start | bytes 1783304 | tf_op jit(solution)/shard_map/ppermute | solution.py:304
  59.1 39.6 %collective-permute-start.5 = (bf16[387,768]{1,0:T(8,128)(2,1)}, bf16[387,768]{1,0:T(8,128)(2,1)}, u32[]{:S(2)}, u32[]{:S(2)}) collective-permute-start(bf16[387,768]{1,0:T(8,128)(2,1)} %collective-permute-done.2), channel_id=1, source_target_pairs={{320,384},{384,448},{448,0},{321,385},{385,449},{449,1},{322,386},... | collective-permute-start | bytes 1783304 | tf_op jit(solution)/shard_map/ppermute | solution.py:312
  60.4 19.7 %collective-permute-start.4 = (bf16[384,768]{1,0:T(8,128)(2,1)}, bf16[384,768]{1,0:T(8,128)(2,1)}, u32[]{:S(2)}, u32[]{:S(2)}) collective-permute-start(bf16[384,768]{1,0:T(8,128)(2,1)} %slice.32), channel_id=1, source_target_pairs={{64,0},{128,448},{192,384},{65,1},{129,449},{193,385},{66,2},{130,... | collective-permute-start | bytes 1769480 | tf_op jit(solution)/shard_map/ppermute | solution.py:311
  62.8 12.9 %collective-permute-start.6 = (f32[48,768]{1,0:T(8,128)S(1)}, f32[48,768]{1,0:T(8,128)S(1)}, u32[]{:S(2)}, u32[]{:S(2)}) collective-permute-start(f32[48,768]{1,0:T(8,128)S(1)} %select_n.72), channel_id=1, source_target_pairs={{0,1},{1,0},{2,3},{3,2},{4,5},{5,4},{6,7},{7,6},{8,9},{9,8},{10,11... | collective-permute-start | bytes 442376 | tf_op jit(solution)/shard_map/ppermute | solution.py:315
  68.5 67.0 %collective-permute-start.11 = (bf16[595,768]{1,0:T(8,128)(2,1)S(1)}, bf16[595,768]{1,0:T(8,128)(2,1)}, u32[]{:S(2)}, u32[]{:S(2)}) collective-permute-start(bf16[595,768]{1,0:T(8,128)(2,1)S(1)} %slice.33), channel_id=1, source_target_pairs={{0,64},{64,128},{128,192},{192,256},{256,320},{320,384},{384,448},... | collective-permute-start | bytes 2741768 | tf_op jit(solution)/shard_map/ppermute | solution.py:310
  117.4 12.4 %copy-start.7 = (s32[3]{0:T(128)S(1)}, s32[3]{0:T(128)}, u32[]{:S(2)}) copy-start(s32[3]{0:T(128)} %param.11) | copy-start | bytes 40
  121.0 14.6 %collective-permute-start.10 = (bf16[2,576,384]{2,1,0:T(8,128)(2,1)}, bf16[2,576,384]{2,1,0:T(8,128)(2,1)}, u32[]{:S(2)}, u32[]{:S(2)}) collective-permute-start(bf16[2,576,384]{2,1,0:T(8,128)(2,1)} %get-tuple-element.36), channel_id=1, source_target_pairs={{0,1},{1,0},{2,3},{3,2},{4,5},{5,4},{6,7},{7,6},{8,9},{9,8},{10,11... | collective-permute-start | bytes 2654216 | tf_op jit(solution)/shard_map/ppermute | solution.py:321
  123.6 12.0 %collective-permute-start.9 = (bf16[2,576,384]{2,1,0:T(8,128)(2,1)}, bf16[2,576,384]{2,1,0:T(8,128)(2,1)}, u32[]{:S(2)}, u32[]{:S(2)}) collective-permute-start(bf16[2,576,384]{2,1,0:T(8,128)(2,1)} %get-tuple-element.37), channel_id=1, source_target_pairs={{0,1},{1,0},{2,3},{3,2},{4,5},{5,4},{6,7},{7,6},{8,9},{9,8},{10,11... | collective-permute-start | bytes 2654216 | tf_op jit(solution)/shard_map/ppermute | solution.py:321
  125.5 10.1 %collective-permute-start.8 = (bf16[2,576,384]{2,1,0:T(8,128)(2,1)}, bf16[2,576,384]{2,1,0:T(8,128)(2,1)}, u32[]{:S(2)}, u32[]{:S(2)}) collective-permute-start(bf16[2,576,384]{2,1,0:T(8,128)(2,1)} %get-tuple-element.38), channel_id=1, source_target_pairs={{0,1},{1,0},{2,3},{3,2},{4,5},{5,4},{6,7},{7,6},{8,9},{9,8},{10,11... | collective-permute-start | bytes 2654216 | tf_op jit(solution)/shard_map/ppermute | solution.py:321
  127.9 7.7 %collective-permute-start.7 = (bf16[2,576,384]{2,1,0:T(8,128)(2,1)S(1)}, bf16[2,576,384]{2,1,0:T(8,128)(2,1)}, u32[]{:S(2)}, u32[]{:S(2)}) collective-permute-start(bf16[2,576,384]{2,1,0:T(8,128)(2,1)S(1)} %get-tuple-element.39), channel_id=1, source_target_pairs={{0,1},{1,0},{2,3},{3,2},{4,5},{5,4},{6,7},{7,6},{8,9},{9,8},{10,11... | collective-permute-start | bytes 2654216 | tf_op jit(solution)/shard_map/ppermute | solution.py:321
  131.2 24.0 %all-to-all-start = ((f32[4,12,768]{2,1,0:T(8,128)}), f32[4,12,768]{2,1,0:T(8,128)S(1)}, u32[]{:S(2)}, u32[]{:S(2)}) async-start(f32[4,12,768]{2,1,0:T(8,128)} %reshape.186), calls=%async_computation.1 | async-start | bytes 393216 | tf_op jit(solution)/shard_map/all_to_all | solution.py:327
Sparse Core Ops, SparseCore 0:
  12.7 48.2 reduce-scatter.1
  63.1 54.3 all-gather.2
